TPU v7x, 128 devices: a whole 4x4x4 slice. The times are simulated.
128 devices in a mesh: row: 16 (over x, y_hi, core), col: 8 (over y_lo, z).
Axes of the slice: x: 4, y: 4 (y_hi: 2, y_lo: 2; y = y_hi * 2 + y_lo), z: 4, core: 2. Of those that a mesh axis runs over, the one named last changes fastest.
Arguments:
- final_amp: bfloat16 [16, 32, 128, 440], P('row', 'col'), may hold values from -0.19921875 to 0.19921875
- initial_amp: bfloat16 [8, 32, 128, 440], P('col', 'row'), may hold values from -0.19921875 to 0.19921875
- pair_final: int32 [16, 8, 128], P('row', 'col'), may hold values from 0 to 31
- pair_initial: int32 [16, 8, 128], P('row', 'col'), may hold values from 0 to 31
- map_final: int32 [16, 32, 440], P('row', 'col'), may hold values from 0 to 439, each once within a row
- map_initial: int32 [8, 32, 440], P('col', 'row'), may hold values from 0 to 439, each once within a row
- counts: int32 [16, 8], P('row', 'col'), may hold values from 16 to 128, as said below
Outputs:
- density: float32 [440, 440], replicated
Inputs may be any that keep to these rules, and one draw needn't show every extreme that they name: `counts`: slots at or past a cell's count are ignored. Exactly one cell of every draw has 128 live slots.
All inputs are finite; a program needn't handle non-finite values.
Results may differ from a plain program's by a relative error of at most 0.0003.
Values may be sent and summed in bfloat16 or wider, within the bound.
No kernel may reach another device: no remote copies, remote signals or barrier semaphores. Data moves between devices by JAX's collectives and lax.ppermute only.
A program may use at most 64 MiB of HBM per device.

v0:
```python
import jax
import jax.numpy as jnp
from jax import lax
from jax.sharding import PartitionSpec as P

GROUP = 32


def permute_columns(blocks, orbital_map):
    return jnp.take(blocks, orbital_map, axis=1)


def shards(final_amp, initial_amp, pair_final, pair_initial, map_final, map_initial, counts):
    own_final = jax.vmap(permute_columns)(final_amp[0], map_final[0])[None]
    own_initial = jax.vmap(permute_columns)(initial_amp[0], map_initial[0])[None]
    row_seg = lax.all_gather(own_final, "col", axis=1, tiled=True)[0]
    column_seg = lax.all_gather(own_initial, "row", axis=1, tiled=True)[0]
    slots_final = pair_final[0, 0]
    slots_initial = pair_initial[0, 0]
    live_count = counts[0, 0]
    orbitals = final_amp.shape[3]
    group_size = GROUP

    def advance(index, summed):
        first_slot = index * group_size
        which_final = lax.dynamic_slice_in_dim(slots_final, first_slot, group_size)
        which_initial = lax.dynamic_slice_in_dim(slots_initial, first_slot, group_size)
        live_mask = first_slot + jnp.arange(group_size, dtype=jnp.int32) < live_count
        left = jnp.take(row_seg, which_final, axis=0)
        right = jnp.take(column_seg, which_initial, axis=0)
        left = jnp.where(live_mask[:, None, None], left, jnp.zeros_like(left))
        product = lax.dot_general(
            left.reshape(-1, orbitals),
            right.reshape(-1, orbitals),
            (((0,), (0,)), ((), ())),
            preferred_element_type=jnp.float32,
        )
        return summed + product

    turns = (live_count + group_size - 1) // group_size
    partial_density = lax.fori_loop(0, turns, advance, jnp.zeros((orbitals, orbitals), jnp.float32))
    density = lax.psum(partial_density, ("row", "col"))
    return density


def solution(mesh):
    placed = (
        P("row", "col", None, None),
        P("col", "row", None, None),
        P("row", "col", None),
        P("row", "col", None),
        P("row", "col", None),
        P("col", "row", None),
        P("row", "col"),
    )
    return jax.shard_map(shards, mesh=mesh, in_specs=placed, out_specs=P(), check_vma=False)
```

profile of v0, /device:TPU:1, one launch (start us, length us, event | category | flops | bytes accessed | tf_op | source)
XLA Modules:
  0.0 356.8 jit_solution(11643161233148590694)
XLA Ops:
  6.5 0.8 compare_and_fusion.3
  7.3 0.7 fusion.17
  8.1 15.7 %gather_fusion.2 = bf16[1760,128]{1,0:T(8,128)(2,1)S(1)} fusion(bf16[4,128,440]{1,2,0:T(8,128)(2,1)S(1)} %bitcast.38, s32[1760]{0:T(1024)S(1)} %reshape.110), kind=kCustom, calls=%fused_computation.2 | custom fusion | bytes 915200 | tf_op jit(solution)/shard_map/vmap(jit(_take))/gather | solution.py:10
  23.8 1.1 broadcast_select_fusion
  25.1 9.2 %gather_fusion.3 = bf16[880,128]{1,0:T(8,128)(2,1)S(1)} fusion(bf16[2,128,440]{1,2,0:T(8,128)(2,1)S(1)} %bitcast.39, s32[880]{0:T(1024)S(1)} %reshape.116), kind=kCustom, calls=%fused_computation.3 | custom fusion | bytes 457600 | tf_op jit(solution)/shard_map/vmap(jit(_take))/gather | solution.py:10
  34.3 0.9 broadcast_select_fusion.1
  35.9 39.7 %all-gather.3.cloned.1.call-done = bf16[1,32,128,440]{2,3,0,1:T(8,128)(2,1)} async-done(((bf16[1,4,128,440]{2,3,0,1:T(8,128)(2,1)}), bf16[1,32,128,440]{2,3,0,1:T(8,128)(2,1)}) %all-gather.3.cloned.1.call-update) | async-done | bytes 3604496 | tf_op jit(solution)/shard_map/all_gather | solution.py:16
  75.6 6.4 %copy.14 = bf16[32,128,440]{2,1,0:T(8,128)(2,1)} copy(bf16[32,128,440]{1,2,0:T(8,128)(2,1)} %bitcast.40) | data formatting | bytes 7208960 | tf_op jit(solution)/shard_map/while | solution.py:41
  82.0 49.4 %all-gather.5.cloned.1.call-done = bf16[1,32,128,440]{2,3,0,1:T(8,128)(2,1)} async-done(((bf16[1,2,128,440]{2,3,0,1:T(8,128)(2,1)}), bf16[1,32,128,440]{2,3,0,1:T(8,128)(2,1)}) %all-gather.5.cloned.1.call-update) | async-done | bytes 3604496 | tf_op jit(solution)/shard_map/all_gather | solution.py:17
  131.5 6.5 %copy.15 = bf16[32,128,440]{2,1,0:T(8,128)(2,1)} copy(bf16[32,128,440]{1,2,0:T(8,128)(2,1)} %bitcast.41) | data formatting | bytes 7208960 | tf_op jit(solution)/shard_map/while | solution.py:41
  137.9 0.1 broadcast_in_dim.43
  138.1 33.5 %while.10 = (s32[]{:T(128)}, f32[440,440]{1,0:T(8,128)S(1)}, s32[]{:T(128)}, s32[]{:T(128)}, s32[128]{0:T(128)S(1)}, /*index=5*/bf16[32,128,440]{2,1,0:T(8,128)(...) while((s32[]{:T(128)}, f32[440,440]{1,0:T(8,128)S(1)}, ...), condition=%wide.region_1.3_spmd, body=%wide.region_0.0_spmd.sunk | while | flops 1591574016 | bytes 23185264 | solution.py:41
  138.1 0.7 add_compare_fusion.2
  138.7 0.1 compare_and_fusion.5
  138.8 4.9 %gather_fusion.1 = bf16[32,128,440]{2,1,0:T(8,128)(2,1)} fusion(bf16[32,128,440]{2,1,0:T(8,128)(2,1)} %get-tuple-element.167, s32[1024]{0:T(1024)S(1)} %pad_clamp_fusion.5), kind=kCustom, calls=%fused_computation.clone.clone.1 | custom fusion | bytes 7209088 | tf_op jit(solution)/shard_map/while/body/jit(_take)/gather | solution.py:29
  143.8 5.0 %gather_fusion = bf16[32,128,440]{2,1,0:T(8,128)(2,1)} fusion(bf16[32,128,440]{2,1,0:T(8,128)(2,1)} %get-tuple-element.169, s32[1024]{0:T(1024)S(1)} %pad_clamp_fusion.4), kind=kCustom, calls=%fused_computation.1.clone.clone.1 | custom fusion | bytes 7209088 | tf_op jit(solution)/shard_map/while/body/jit(_take)/gather | solution.py:30
  148.7 6.1 %fusion.24 = f32[440,440]{1,0:T(8,128)S(1)} fusion(f32[440,440]{1,0:T(8,128)S(1)} %get-tuple-element.151, bf16[32,128,440]{2,1,0:T(8,128)(2,1)} %gather_fusion, pred[32]{0:T(512)(128)(4,1)S(1)} %get-tuple-element.135, bf16[32,128,440]{2,1,0:T(8,128)(2,1)} %gather_fusion.1, pred[32]{0:T(512)(128)(4,1)S(1)} %get-tuple-element.137, ...), kind=kOutput, calls=%fused_computation.13.clone.1 | convolution fusion | flops 1591571456 | bytes 8757856 | tf_op jit(solution)/shard_map/while/body/dot_general | solution.py:32
  154.8 0.7 add_compare_fusion.2
  155.6 4.9 %gather_fusion.1 = bf16[32,128,440]{2,1,0:T(8,128)(2,1)} fusion(bf16[32,128,440]{2,1,0:T(8,128)(2,1)} %get-tuple-element.167, s32[1024]{0:T(1024)S(1)} %pad_clamp_fusion.5), kind=kCustom, calls=%fused_computation.clone.clone.1 | custom fusion | bytes 7209088 | tf_op jit(solution)/shard_map/while/body/jit(_take)/gather | solution.py:29
  160.5 5.0 %gather_fusion = bf16[32,128,440]{2,1,0:T(8,128)(2,1)} fusion(bf16[32,128,440]{2,1,0:T(8,128)(2,1)} %get-tuple-element.169, s32[1024]{0:T(1024)S(1)} %pad_clamp_fusion.4), kind=kCustom, calls=%fused_computation.1.clone.clone.1 | custom fusion | bytes 7209088 | tf_op jit(solution)/shard_map/while/body/jit(_take)/gather | solution.py:30
  165.5 6.0 %fusion.24 = f32[440,440]{1,0:T(8,128)S(1)} fusion(f32[440,440]{1,0:T(8,128)S(1)} %get-tuple-element.151, bf16[32,128,440]{2,1,0:T(8,128)(2,1)} %gather_fusion, pred[32]{0:T(512)(128)(4,1)S(1)} %get-tuple-element.135, bf16[32,128,440]{2,1,0:T(8,128)(2,1)} %gather_fusion.1, pred[32]{0:T(512)(128)(4,1)S(1)} %get-tuple-element.137, ...), kind=kOutput, calls=%fused_computation.13.clone.1 | convolution fusion | flops 1591571456 | bytes 8757856 | tf_op jit(solution)/shard_map/while/body/dot_general | solution.py:32
  171.6 0.9 copy-done.2
  172.5 175.6 %all-reduce.2.cloned.1.call-done = f32[440,440]{1,0:T(8,128)} async-done(((f32[440,440]{1,0:T(8,128)}), f32[440,440]{1,0:T(8,128)}) %all-reduce.2.cloned.1.call-update) | async-done | bytes 774416 | tf_op jit(solution)/shard_map/psum | solution.py:42
  348.1 2.1 copy.26
  (26 shorter events, 0.4 us)
Async XLA Ops:
  6.5 1.6 copy-start
  6.5 18.4 %copy-start.3 = (s32[1,2,440]{2,1,0:T(2,128)S(1)}, s32[1,2,440]{2,1,0:T(2,128)}, u32[]{:S(2)}) copy-start(s32[1,2,440]{2,1,0:T(2,128)} %param.16) | copy-start | bytes 10564
  6.5 18.6 %copy-start.1 = (bf16[1,2,128,440]{2,3,1,0:T(8,128)(2,1)S(1)}, bf16[1,2,128,440]{2,3,1,0:T(8,128)(2,1)}, u32[]{:S(2)}) copy-start(bf16[1,2,128,440]{2,3,1,0:T(8,128)(2,1)} %param.12) | copy-start | bytes 675844
  6.5 69.0 %all-gather.3.cloned.1.call-start = ((), (), s32[]{:S(2)}) async-start(), calls=%async_computation | async-start | bytes 4055040 | tf_op jit(solution)/shard_map/all_gather | solution.py:16
  24.9 106.5 %all-gather.5.cloned.1.call-start = ((), (), s32[]{:S(2)}) async-start(), calls=%async_computation.1 | async-start | bytes 3829760 | tf_op jit(solution)/shard_map/all_gather | solution.py:17
  35.2 312.9 %all-reduce.2.cloned.1.call-start = ((), (), s32[]{:S(2)}) async-start(), calls=%async_computation.2 | async-start | bytes 1802240 | tf_op jit(solution)/shard_map/psum | solution.py:42
  131.5 6.6 %copy-start.4 = (s32[1,1,128]{2,1,0:T(1,128)S(1)}, s32[1,1,128]{2,1,0:T(1,128)}, u32[]{:S(2)}) copy-start(s32[1,1,128]{2,1,0:T(1,128)} %param.13) | copy-start | bytes 1540
  131.5 6.6 %copy-start.5 = (s32[1,1,128]{2,1,0:T(1,128)S(1)}, s32[1,1,128]{2,1,0:T(1,128)}, u32[]{:S(2)}) copy-start(s32[1,1,128]{2,1,0:T(1,128)} %param.14) | copy-start | bytes 1540
  171.6 0.9 copy-start.2
Sparse Core Ops, SparseCore 0:
  25.1 50.4 all-gather.2
  77.9 53.5 all-gather.4
  172.6 175.4 all-reduce.1
where the time goes:
time: 358 us; the launch traced here: 357 us
  waiting for transfers between devices  265 us (74%)
  local copies, waits for them, and re-layouts  60.9 us (17%)
  between operations  13.9 us (4%)
  matrix products  12.1 us (3%)
  other arithmetic  4.94 us (1%)
    psum x1, waiting for transfers between devices, shards(): density = lax.psum(partial_density, ('row', 'col'))  176 us
    all_gather x1, waiting for transfers between devices, shards(): column_seg = lax.all_gather(own_initial, 'row', axis=1, tiled=True)[0]  49.4 us
    all_gather x1, waiting for transfers between devices, shards(): row_seg = lax.all_gather(own_final, 'col', axis=1, tiled=True)[0]  39.7 us
    gather x4, local copies, waits for them, and re-layouts, permute_columns(): return jnp.take(blocks, orbital_map, axis=1)  25.1 us
    while x2, local copies, waits for them, and re-layouts, shards(): lax.fori_loop(0, turns, advance, jnp.zeros((orbitals, orbitals), jnp.floa...  12.9 us
    dot_general x2, matrix products, advance(): lax.dot_general(left.reshape(-1, orbitals), right.reshape(-1, orbitals),...  12.1 us
    gather x2, local copies, waits for them, and re-layouts, advance(): right = jnp.take(column_seg, which_initial, axis=0)  9.93 us
    gather x2, local copies, waits for them, and re-layouts, advance(): left = jnp.take(row_seg, which_final, axis=0)  9.86 us
  transfers between devices with their start and end apart: 3, of which 3 were waited for; matrix products, arithmetic and copies ran while one was open for 5% of the time, Pallas kernels for 0%

commit v1 on v0

v1 whole, which is shorter than its diff:
```python
import jax
import jax.numpy as jnp
from jax import lax
from jax.experimental import pallas as pl
from jax.experimental.pallas import tpu as pltpu
from jax.sharding import PartitionSpec as P

LANES = 128
DEVICES = 128
FINAL_ROWS = 16
MESSAGE = 24
SLICE = 12
STRIPS = 55
HALF = 27
TAIL = 56
DEAD = 64
AXES = ("row", "col")
PARAMS = pltpu.CompilerParams(vmem_limit_bytes=48 * 1024 * 1024)


def lane_index(shape):
    return lax.broadcasted_iota(jnp.int32, shape, len(shape) - 1)


def send_kernel(count_ref, final_ref, initial_ref, pf_ref, pi_ref, mf_ref, mi_ref, out_ref, maps, wide):
    maps[...] = jnp.full(maps.shape, -1, jnp.int32)
    maps[0:4, 0:440] = mf_ref[0]
    maps[4:6, 0:440] = mi_ref[0]
    slot = lane_index((1, LANES))
    q = pf_ref[0]
    s = pi_ref[0]
    q_code = jnp.where(slot < count_ref[0, 0], (q & 3) * 8 + (q >> 2), DEAD).astype(jnp.float32)
    s_code = ((s & 1) * LANES + (s >> 1) * 8).astype(jnp.float32)
    q_code = jnp.broadcast_to(q_code, (8, LANES))
    s_code = jnp.broadcast_to(s_code, (8, LANES))
    info = [pltpu.roll(q_code, 64, 1), q_code, pltpu.roll(s_code, 64, 1), s_code]
    upper = lane_index((LANES, LANES)) >= 64
    for j in range(6):
        block = final_ref[0, j] if j < 4 else initial_ref[0, j - 4]
        stored = lax.broadcasted_iota(jnp.int32, (440, 512), 0)
        pick = jnp.where(stored == maps[j : j + 1, :], 1.0, 0.0).astype(jnp.bfloat16)
        ordered = jnp.dot(block, pick, preferred_element_type=jnp.float32)
        for chunk in range(4):
            part = ordered[:, chunk * LANES : (chunk + 1) * LANES]
            if chunk == 3 and j < 4:
                part = jnp.where(upper, jnp.broadcast_to(info[j][0:1], (LANES, LANES)), part)
            wide[pl.ds(j * 4 + chunk, DEVICES, stride=MESSAGE), :] = part
    out_ref[...] = wide[...].astype(jnp.bfloat16)


def density_kernel(in_ref, out_ref, wide, pairs, final, initial, full):
    wide[...] = in_ref[...].astype(jnp.float32)

    def rows(r):
        return wide[pl.ds(r, DEVICES, stride=MESSAGE), :]

    lower = lane_index((LANES, LANES)) < 64
    codes = [
        jnp.where(lower, pltpu.roll(rows(3 + 8 * k), 64, 1), rows(7 + 8 * k)).astype(jnp.int32) for k in range(2)
    ]
    pairs[0:LANES, :] = codes[0]
    pairs[LANES:, :] = codes[1] + (lax.broadcasted_iota(jnp.int32, (LANES, LANES), 0) & 7)

    for j in range(4):
        for chunk in range(4):
            final[j * LANES : (j + 1) * LANES, chunk * LANES : (chunk + 1) * LANES] = rows(j * 4 + chunk).astype(jnp.bfloat16)
    for j in range(2):
        for chunk in range(4):
            part = rows(FINAL_ROWS + j * 4 + chunk).astype(jnp.bfloat16)
            initial[j * LANES : (j + 1) * LANES, chunk * LANES : (chunk + 1) * LANES] = part
            initial[(2 + j) * LANES : (3 + j) * LANES, chunk * LANES : (chunk + 1) * LANES] = part

    def count(r, carry):
        q = pairs[pl.ds(pl.multiple_of(r * 8, 8), 8), :]
        s = pairs[pl.ds(pl.multiple_of(LANES + r * 8, 8), 8), :]
        final_is = lax.broadcasted_iota(jnp.int32, (32, LANES), 0)
        initial_is = lax.broadcasted_iota(jnp.int32, (256, LANES), 0)
        left = jnp.concatenate([jnp.where(final_is == q[c : c + 1], 1.0, 0.0) for c in range(8)], axis=1)
        right = jnp.concatenate([jnp.where(initial_is == s[c : c + 1], 1.0, 0.0) for c in range(8)], axis=1)
        met = lax.dot_general(
            left.astype(jnp.bfloat16),
            right.astype(jnp.bfloat16),
            (((1,), (1,)), ((), ())),
            preferred_element_type=jnp.float32,
        )
        for j in range(4):
            full[pl.ds(pl.multiple_of(j * LANES + r * 8, 8), 8), 0:256] = met[j * 8 : (j + 1) * 8]
        return carry

    lax.fori_loop(0, 16, count, 0)
    met = full[:, 0:256].astype(jnp.bfloat16)
    across = (((0,), (0,)), ((), ()))
    summed = lax.dot_general(met, final[...], across, preferred_element_type=jnp.float32)
    high = summed.astype(jnp.bfloat16)
    low = (summed - high.astype(jnp.float32)).astype(jnp.bfloat16)
    full[...] = lax.dot_general(
        jnp.concatenate([high, low], axis=0), initial[...], across, preferred_element_type=jnp.float32
    )

    lane = lane_index((8, LANES))

    def tile(e, chunk):
        return full[e * 8 : (e + 1) * 8, chunk * LANES : (chunk + 1) * LANES]

    for e in range(STRIPS):
        for chunk in range(3):
            t = e * 3 + chunk
            out_ref[t * 8 : (t + 1) * 8, :] = tile(e, chunk)
    last = tile(STRIPS - 1, 3)
    for e in range(HALF):
        t = STRIPS * 3 + e
        packed = jnp.where(lane < 64, tile(e, 3), pltpu.roll(tile(e + HALF, 3), 64, 1))
        if e < 7:
            packed = jnp.where((lane >= TAIL) & (lane < 64), pltpu.roll(last, TAIL - 8 * e, 1), packed)
        out_ref[t * 8 : (t + 1) * 8, :] = packed


def sum_kernel(in_ref, out_ref):
    total = in_ref[0:24, :]
    for d in range(1, DEVICES // 2):
        total = total + in_ref[d * 24 : (d + 1) * 24, :]
    own = total[0:SLICE] + total[SLICE:24]
    twice = jnp.concatenate([own, own], axis=0)
    for d in range(DEVICES // 2):
        out_ref[d * 24 : (d + 1) * 24, :] = twice


def place_kernel(in_ref, out_ref):
    def tile(t):
        return in_ref[t * 8 : (t + 1) * 8, :]

    lane = lane_index((8, LANES))
    for e in range(STRIPS):
        for chunk in range(3):
            out_ref[e * 8 : (e + 1) * 8, chunk * LANES : (chunk + 1) * LANES] = tile(e * 3 + chunk)
        if e < HALF:
            strip = tile(STRIPS * 3 + e)
        elif e < STRIPS - 1:
            strip = pltpu.roll(tile(STRIPS * 3 + e - HALF), 64, 1)
        else:
            strip = jnp.zeros((8, LANES), jnp.float32)
            for k in range(7):
                piece = pltpu.roll(tile(STRIPS * 3 + k), (8 * k - TAIL) % LANES, 1)
                strip = jnp.where((lane >= 8 * k) & (lane < 8 * k + 8), piece, strip)
        out_ref[e * 8 : (e + 1) * 8, 3 * LANES : 440] = strip[:, 0:TAIL]


def exchange(x, shape):
    return lax.all_to_all(x.reshape((DEVICES,) + shape), AXES, 0, 0, tiled=True).reshape(x.shape)


def shards(final_amp, initial_amp, pair_final, pair_initial, map_final, map_initial, counts):
    vmem = pl.BlockSpec(memory_space=pltpu.VMEM)
    smem = pl.BlockSpec(memory_space=pltpu.SMEM)
    f32, bf16 = jnp.float32, jnp.bfloat16
    messages = pl.pallas_call(
        send_kernel,
        out_shape=jax.ShapeDtypeStruct((DEVICES * MESSAGE, LANES), bf16),
        in_specs=[smem] + [vmem] * 6,
        out_specs=vmem,
        scratch_shapes=[pltpu.VMEM((8, 512), jnp.int32), pltpu.VMEM((DEVICES * MESSAGE, LANES), f32)],
        compiler_params=PARAMS,
    )(counts, final_amp, initial_amp, pair_final, pair_initial, map_final, map_initial)
    received = exchange(messages, (MESSAGE, LANES))
    share = pl.pallas_call(
        density_kernel,
        out_shape=jax.ShapeDtypeStruct((DEVICES * SLICE, LANES), f32),
        in_specs=[vmem],
        out_specs=vmem,
        scratch_shapes=[
            pltpu.VMEM((DEVICES * MESSAGE, LANES), f32),
            pltpu.VMEM((2 * LANES, LANES), jnp.int32),
            pltpu.VMEM((512, 512), bf16),
            pltpu.VMEM((512, 512), bf16),
            pltpu.VMEM((512, 512), f32),
        ],
        compiler_params=PARAMS,
    )(received)
    shares = exchange(share, (3, 4, LANES))
    copies = pl.pallas_call(
        sum_kernel,
        out_shape=jax.ShapeDtypeStruct((DEVICES * SLICE, LANES), f32),
        in_specs=[vmem],
        out_specs=vmem,
        compiler_params=PARAMS,
    )(shares)
    slices = exchange(copies, (3, 4, LANES))
    return pl.pallas_call(
        place_kernel,
        out_shape=jax.ShapeDtypeStruct((440, 440), f32),
        in_specs=[vmem],
        out_specs=vmem,
        compiler_params=PARAMS,
    )(slices)


def solution(mesh):
    placed = (
        P("row", "col", None, None),
        P("col", "row", None, None),
        P("row", "col", None),
        P("row", "col", None),
        P("row", "col", None),
        P("col", "row", None),
        P("row", "col"),
    )
    return jax.shard_map(shards, mesh=mesh, in_specs=placed, out_specs=P(), check_vma=False)
```

time: 358 us -> 79.5 us (0.22)
  waiting for transfers between devices: 265 us -> 0 us
  blocking collectives: 0 us -> 69.2 us
  local copies, waits for them, and re-layouts: 60.9 us -> 1.78 us
  between operations: 13.9 us -> 0.78 us
  matrix products: 12.1 us -> 0 us
  Pallas kernels: 0 us -> 7.51 us
  other arithmetic: 4.94 us -> 0 us
    psum x1 -> x0, waiting for transfers between devices: 176 us -> none  [shards(): density = lax.psum(partial_density, ('row', 'col'))]
    all_gather x2 -> x0, waiting for transfers between devices: 89.1 us -> none  [the longest x1 49.4 us: shards(): column_seg = lax.all_gather(own_initial, 'row', axis=1, tiled=True)[0]]
    all_to_all x0 -> x3, blocking collectives: none -> 69.2 us  [exchange(): lax.all_to_all(x.reshape((DEVICES,) + shape), AXES, 0, 0, tiled=True)]
    gather x8 -> x0, local copies, waits for them, and re-layouts: 44.9 us -> none  [the longest x4 25.1 us: permute_columns(): return jnp.take(blocks, orbital_map, axis=1)]
    while x2 -> x0, local copies, waits for them, and re-layouts: 12.9 us -> none  [shards(): lax.fori_loop(0, turns, advance, jnp.zeros((orbitals, orbitals), jnp.floa...]
    dot_general x2 -> x0, matrix products: 12.1 us -> none  [advance(): lax.dot_general(left.reshape(-1, orbitals), right.reshape(-1, orbitals),...]
    pallas_call x0 -> x4, Pallas kernels: none -> 7.51 us  [the longest x1 5.65 us: shards(): pl.pallas_call(density_kernel, out_shape=jax.ShapeDtypeStruct((DEVICES *...]
  transfers between devices with their start and end apart: 3 -> 0, of which waited for: 3 -> 0; matrix products, arithmetic and copies ran while one was open for 5% -> 0% of each run, Pallas kernels for 0% -> 0%
where the time goes in v1:
time: 79.5 us; the launch traced here: 79.2 us
  blocking collectives  69.2 us (87%)
  Pallas kernels  7.51 us (9%)
  local copies, waits for them, and re-layouts  1.78 us (2%)
    all_to_all x3, blocking collectives, exchange(): lax.all_to_all(x.reshape((DEVICES,) + shape), AXES, 0, 0, tiled=True)  69.2 us
    pallas_call x1, Pallas kernels, shards(): pl.pallas_call(density_kernel, out_shape=jax.ShapeDtypeStruct((DEVICES *...  5.65 us
    unnamed x12, local copies, waits for them, and re-layouts  1.78 us

profile of v1, /device:TPU:1, one launch (start us, length us, event | category | flops | bytes accessed | tf_op | source)
XLA Modules:
  0.0 79.2 jit_solution(17404669662243747597)
XLA Ops:
  0.0 0.0 copy-start.4
  0.7 1.1 %copy.9.initial_ref = bf16[1,2,128,440]{3,2,1,0:T(8,128)(2,1)S(1)} copy(bf16[1,2,128,440]{2,3,1,0:T(8,128)(2,1)} %param.8) | data formatting | bytes 450560 | tf_op args[1]
  1.8 0.0 copy-done.4
  1.8 0.0 copy-start
  1.8 0.0 copy-start.1
  1.9 0.0 copy-start.2
  1.9 0.0 copy-start.3
  1.9 0.2 copy.8.final_ref
  2.1 0.4 copy-done
  2.5 0.0 copy-done.1
  2.5 0.0 copy-done.2
  2.5 0.0 copy-done.3
  2.5 0.7 shard_map.73
  3.3 28.0 %all_to_all.15 = bf16[128,24,128]{2,1,0:T(8,128)(2,1)S(1)} all-to-all(bf16[128,24,128]{2,1,0:T(8,128)(2,1)S(1)} %bitcast.6), channel_id=1, replica_groups=mesh['row'=16,'col'=8] {'row','col'}, dimensions={0} | all-to-all | bytes 1572864 | tf_op jit(solution)/shard_map/all_to_all | solution.py:149
  31.3 5.6 %shard_map.74 = f32[1536,128]{1,0:T(8,128)S(1)} custom-call(bf16[3072,128]{1,0:T(8,128)(2,1)S(1)} %bitcast.7), custom_call_target="tpu_custom_call" | custom-call | tf_op jit(solution)/shard_map/pallas_call | solution.py:165
  37.0 20.6 %all_to_all.16 = f32[128,3,4,128]{3,2,1,0:T(4,128)S(1)} all-to-all(f32[128,3,4,128]{3,2,1,0:T(4,128)S(1)} %bitcast.8), channel_id=1, replica_groups=mesh['row'=16,'col'=8] {'row','col'}, dimensions={0} | all-to-all | bytes 1572864 | tf_op jit(solution)/shard_map/all_to_all | solution.py:149
  57.5 0.1 shard_map.75
  57.7 20.6 %all_to_all.17 = f32[128,3,4,128]{3,2,1,0:T(4,128)S(1)} all-to-all(f32[128,3,4,128]{3,2,1,0:T(4,128)S(1)} %bitcast.10), channel_id=1, replica_groups=mesh['row'=16,'col'=8] {'row','col'}, dimensions={0} | all-to-all | bytes 1572864 | tf_op jit(solution)/shard_map/all_to_all | solution.py:149
  78.2 1.0 %shard_map.76 = f32[440,440]{1,0:T(8,128)} custom-call(f32[1536,128]{1,0:T(8,128)S(1)} %bitcast.11), custom_call_target="tpu_custom_call" | custom-call | tf_op jit(solution)/shard_map/pallas_call | solution.py:188
Async XLA Ops:
  0.0 1.8 %copy-start.4 = (bf16[1,4,128,440]{2,3,1,0:T(8,128)(2,1)S(1)}, bf16[1,4,128,440]{2,3,1,0:T(8,128)(2,1)}, u32[]{:S(2)}) copy-start(bf16[1,4,128,440]{2,3,1,0:T(8,128)(2,1)} %param.7) | copy-start | bytes 1351684
  1.8 0.7 copy-start
  1.8 0.7 copy-start.1
  1.9 0.7 copy-start.2
  1.9 0.7 copy-start.3

commit v2 on v1

v2 whole, which is shorter than its diff:
```python
import jax
import jax.numpy as jnp
from jax import lax
from jax.experimental import pallas as pl
from jax.experimental.pallas import tpu as pltpu
from jax.sharding import Mesh
from jax.sharding import PartitionSpec as P

LANES = 128
DEVICES = 128
CHIPS = 64
FINAL_ROWS = 16
MESSAGE = 24
SLICE = 12
TILES = 192
STRIPS = 55
HALF = 27
TAIL = 56
DEAD = 64
ALL = ("x", "y_hi", "core", "y_lo", "z")
ACROSS_CHIPS = ("x", "y_hi", "y_lo", "z")
PARAMS = pltpu.CompilerParams(vmem_limit_bytes=48 * 1024 * 1024)


def lane_index(shape):
    return lax.broadcasted_iota(jnp.int32, shape, len(shape) - 1)


def send_kernel(count_ref, final_ref, initial_ref, pf_ref, pi_ref, mf_ref, mi_ref, out_ref, maps, wide):
    maps[...] = jnp.full(maps.shape, -1, jnp.int32)
    maps[0:4, 0:440] = mf_ref[0]
    maps[4:6, 0:440] = mi_ref[0]
    slot = lane_index((1, LANES))
    q = pf_ref[0]
    s = pi_ref[0]
    q_code = jnp.where(slot < count_ref[0, 0], (q & 3) * 8 + (q >> 2), DEAD).astype(jnp.float32)
    s_code = ((s & 1) * LANES + (s >> 1) * 8).astype(jnp.float32)
    q_code = jnp.broadcast_to(q_code, (8, LANES))
    s_code = jnp.broadcast_to(s_code, (8, LANES))
    info = [pltpu.roll(q_code, 64, 1), q_code, pltpu.roll(s_code, 64, 1), s_code]
    upper = lane_index((LANES, LANES)) >= 64
    for j in range(6):
        block = final_ref[0, j] if j < 4 else initial_ref[0, j - 4]
        stored = lax.broadcasted_iota(jnp.int32, (440, 512), 0)
        pick = jnp.where(stored == maps[j : j + 1, :], 1.0, 0.0).astype(jnp.bfloat16)
        ordered = lax.dot_general(block, pick, (((0,), (0,)), ((), ())), preferred_element_type=jnp.float32)
        for chunk in range(4):
            part = ordered[:, chunk * LANES : (chunk + 1) * LANES]
            if chunk == 3 and j < 4:
                part = jnp.where(upper, jnp.broadcast_to(info[j][0:1], (LANES, LANES)), part)
            wide[pl.ds(j * 4 + chunk, DEVICES, stride=MESSAGE), :] = part
    out_ref[...] = wide[...].astype(jnp.bfloat16)


def density_kernel(in_ref, keep_ref, give_ref, wide, pairs, final, initial, full):
    wide[...] = in_ref[...].astype(jnp.float32)

    def rows(r):
        return wide[pl.ds(r, DEVICES, stride=MESSAGE), :]

    lower = lane_index((LANES, LANES)) < 64
    codes = [
        jnp.where(lower, pltpu.roll(rows(3 + 8 * k), 64, 1), rows(7 + 8 * k)).astype(jnp.int32) for k in range(2)
    ]
    pairs[0:LANES, :] = codes[0]
    pairs[LANES:, :] = codes[1] + (lax.broadcasted_iota(jnp.int32, (LANES, LANES), 0) & 7)

    for j in range(4):
        for chunk in range(4):
            final[j * LANES : (j + 1) * LANES, chunk * LANES : (chunk + 1) * LANES] = rows(j * 4 + chunk).astype(jnp.bfloat16)
    for j in range(2):
        for chunk in range(4):
            part = rows(FINAL_ROWS + j * 4 + chunk).astype(jnp.bfloat16)
            initial[j * LANES : (j + 1) * LANES, chunk * LANES : (chunk + 1) * LANES] = part
            initial[(2 + j) * LANES : (3 + j) * LANES, chunk * LANES : (chunk + 1) * LANES] = part

    final_is = lax.broadcasted_iota(jnp.int32, (32, LANES), 0)
    initial_is = lax.broadcasted_iota(jnp.int32, (256, LANES), 0)
    for r in range(16):
        q = pairs[r * 8 : r * 8 + 8, :]
        s = pairs[LANES + r * 8 : LANES + r * 8 + 8, :]
        left = jnp.concatenate([jnp.where(final_is == q[c : c + 1], 1.0, 0.0) for c in range(8)], axis=1)
        right = jnp.concatenate([jnp.where(initial_is == s[c : c + 1], 1.0, 0.0) for c in range(8)], axis=1)
        met = lax.dot_general(
            left.astype(jnp.bfloat16),
            right.astype(jnp.bfloat16),
            (((1,), (1,)), ((), ())),
            preferred_element_type=jnp.float32,
        )
        for j in range(4):
            full[j * LANES + r * 8 : j * LANES + r * 8 + 8, 0:256] = met[j * 8 : (j + 1) * 8]

    met = full[:, 0:256].astype(jnp.bfloat16)
    across = (((0,), (0,)), ((), ()))
    summed = lax.dot_general(met, final[...], across, preferred_element_type=jnp.float32)
    high = summed.astype(jnp.bfloat16)
    low = (summed - high.astype(jnp.float32)).astype(jnp.bfloat16)
    full[...] = lax.dot_general(
        jnp.concatenate([high, low], axis=0), initial[...], across, preferred_element_type=jnp.float32
    )

    lane = lane_index((8, LANES))

    def tile(e, chunk):
        return full[e * 8 : (e + 1) * 8, chunk * LANES : (chunk + 1) * LANES]

    def packed(t):
        if t < STRIPS * 3:
            return tile(t // 3, t % 3)
        e = t - STRIPS * 3
        two = jnp.where(lane < 64, tile(e, 3), pltpu.roll(tile(e + HALF, 3), 64, 1))
        if e < 7:
            two = jnp.where((lane >= TAIL) & (lane < 64), pltpu.roll(tile(STRIPS - 1, 3), TAIL - 8 * e, 1), two)
        return two

    def split(first, second):
        for t in range(TILES // 2):
            first[t * 8 : (t + 1) * 8, :] = packed(t)
            second[t * 8 : (t + 1) * 8, :] = packed(t + TILES // 2)

    core = lax.axis_index("core")
    pl.when(core == 0)(lambda: split(keep_ref, give_ref))
    pl.when(core == 1)(lambda: split(give_ref, keep_ref))


def add_kernel(a_ref, b_ref, out_ref):
    out_ref[...] = a_ref[...] + b_ref[...]


def sum_kernel(in_ref, out_ref):
    total = in_ref[0:24, :]
    for d in range(1, CHIPS // 2):
        total = total + in_ref[d * 24 : (d + 1) * 24, :]
    own = total[0:SLICE] + total[SLICE:24]
    twice = jnp.concatenate([own, own], axis=0)
    for d in range(CHIPS // 2):
        out_ref[d * 24 : (d + 1) * 24, :] = twice


def place_kernel(kept_ref, given_ref, out_ref):
    lane = lane_index((8, LANES))

    def place(first, second):
        def tile(t):
            half, t = (first, t) if t < TILES // 2 else (second, t - TILES // 2)
            return half[t * 8 : (t + 1) * 8, :]

        for e in range(STRIPS):
            for chunk in range(3):
                out_ref[e * 8 : (e + 1) * 8, chunk * LANES : (chunk + 1) * LANES] = tile(e * 3 + chunk)
            if e < HALF:
                strip = tile(STRIPS * 3 + e)
            elif e < STRIPS - 1:
                strip = pltpu.roll(tile(STRIPS * 3 + e - HALF), 64, 1)
            else:
                strip = jnp.zeros((8, LANES), jnp.float32)
                for k in range(7):
                    piece = pltpu.roll(tile(STRIPS * 3 + k), (8 * k - TAIL) % LANES, 1)
                    strip = jnp.where((lane >= 8 * k) & (lane < 8 * k + 8), piece, strip)
            out_ref[e * 8 : (e + 1) * 8, 3 * LANES : 440] = strip[:, 0:TAIL]

    core = lax.axis_index("core")
    pl.when(core == 0)(lambda: place(kept_ref, given_ref))
    pl.when(core == 1)(lambda: place(given_ref, kept_ref))


def exchange(x, axes, shape):
    return lax.all_to_all(x.reshape(shape), axes, 0, 0, tiled=True).reshape(x.shape)


def to_other_core(x):
    return lax.ppermute(x, "core", [(0, 1), (1, 0)])


def shards(final_amp, initial_amp, pair_final, pair_initial, map_final, map_initial, counts):
    vmem = pl.BlockSpec(memory_space=pltpu.VMEM)
    smem = pl.BlockSpec(memory_space=pltpu.SMEM)
    f32, bf16 = jnp.float32, jnp.bfloat16
    half = jax.ShapeDtypeStruct((CHIPS * SLICE, LANES), f32)

    def call(kernel, out_shape, n, scratch=()):
        several = isinstance(out_shape, list)
        return pl.pallas_call(
            kernel,
            out_shape=out_shape,
            in_specs=[vmem] * n,
            out_specs=[vmem] * len(out_shape) if several else vmem,
            scratch_shapes=list(scratch),
            compiler_params=PARAMS,
        )

    messages = pl.pallas_call(
        send_kernel,
        out_shape=jax.ShapeDtypeStruct((DEVICES * MESSAGE, LANES), bf16),
        in_specs=[smem] + [vmem] * 6,
        out_specs=vmem,
        scratch_shapes=[pltpu.VMEM((8, 512), jnp.int32), pltpu.VMEM((DEVICES * MESSAGE, LANES), f32)],
        compiler_params=PARAMS,
    )(
        counts,
        jnp.swapaxes(final_amp, 2, 3),
        jnp.swapaxes(initial_amp, 2, 3),
        pair_final,
        pair_initial,
        map_final,
        map_initial,
    )
    received = exchange(messages, ALL, (DEVICES, MESSAGE, LANES))
    keep, give = call(
        density_kernel,
        [half, half],
        1,
        [
            pltpu.VMEM((DEVICES * MESSAGE, LANES), f32),
            pltpu.VMEM((2 * LANES, LANES), jnp.int32),
            pltpu.VMEM((512, 512), bf16),
            pltpu.VMEM((512, 512), bf16),
            pltpu.VMEM((512, 512), f32),
        ],
    )(received)
    share = call(add_kernel, half, 2)(keep, to_other_core(give))
    shares = exchange(share, ACROSS_CHIPS, (CHIPS, 3, 4, LANES))
    copies = call(sum_kernel, half, 1)(shares)
    slices = exchange(copies, ACROSS_CHIPS, (CHIPS, 3, 4, LANES))
    return call(place_kernel, jax.ShapeDtypeStruct((440, 440), f32), 2)(slices, to_other_core(slices))


def solution(mesh):
    cores = Mesh(mesh.devices.reshape(4, 2, 2, 2, 4), ALL)
    row, col = ("x", "y_hi", "core"), ("y_lo", "z")
    placed = (
        P(row, col, None, None),
        P(col, row, None, None),
        P(row, col, None),
        P(row, col, None),
        P(row, col, None),
        P(col, row, None),
        P(row, col),
    )
    return jax.shard_map(shards, mesh=cores, in_specs=placed, out_specs=P(), check_vma=False)
```

time: 79.5 us -> 74.3 us (0.935)
  blocking collectives: 69.2 us -> 57.7 us
  starting transfers between devices: 0 us -> 3.95 us
  waiting for transfers between devices: 0 us -> 2.7 us
  Pallas kernels: 7.51 us -> 5.63 us
  local copies, waits for them, and re-layouts: 1.78 us -> 3.3 us
    all_to_all x3, blocking collectives: 69.2 us -> 57.7 us  [exchange(): lax.all_to_all(x.reshape(shape), axes, 0, 0, tiled=True).reshape(x.shape)]
    ppermute x0 -> x2, starting transfers between devices: none -> 3.95 us  [to_other_core(): return lax.ppermute(x, 'core', [(0, 1), (1, 0)])]
    ppermute x0 -> x2, waiting for transfers between devices: none -> 2.7 us  [to_other_core(): return lax.ppermute(x, 'core', [(0, 1), (1, 0)])]
    pallas_call x3 -> x4, Pallas kernels: 6.79 us -> 4.84 us  [the longest x1 3.71 us: shards(): call(density_kernel, [half, half], 1, [pltpu.VMEM((DEVICES * MESSAGE, LAN...]
    unnamed x12, local copies, waits for them, and re-layouts: 1.78 us -> 3.3 us
  transfers between devices with their start and end apart: 0 -> 2, of which waited for: 0 -> 2; matrix products, arithmetic and copies ran while one was open for 0% -> 0% of each run, Pallas kernels for 0% -> 0%
where the time goes in v2:
time: 74.3 us; the launch traced here: 74 us
  blocking collectives  57.7 us (78%)
  Pallas kernels  5.63 us (8%)
  starting transfers between devices  3.95 us (5%)
  local copies, waits for them, and re-layouts  3.3 us (4%)
  waiting for transfers between devices  2.7 us (4%)
    all_to_all x3, blocking collectives, exchange(): lax.all_to_all(x.reshape(shape), axes, 0, 0, tiled=True).reshape(x.shape)  57.7 us
    ppermute x2, starting transfers between devices, to_other_core(): return lax.ppermute(x, 'core', [(0, 1), (1, 0)])  3.95 us
    pallas_call x1, Pallas kernels, shards(): call(density_kernel, [half, half], 1, [pltpu.VMEM((DEVICES * MESSAGE, LAN...  3.71 us
    unnamed x12, local copies, waits for them, and re-layouts  3.3 us
    ppermute x2, waiting for transfers between devices, to_other_core(): return lax.ppermute(x, 'core', [(0, 1), (1, 0)])  2.7 us
  transfers between devices with their start and end apart: 2, of which 2 were waited for; matrix products, arithmetic and copies ran while one was open for 0% of the time, Pallas kernels for 0%

profile of v2, /device:TPU:1, one launch (start us, length us, event | category | flops | bytes accessed | tf_op | source)
XLA Modules:
  0.0 74.0 jit_solution(9369125105106355604)
XLA Ops:
  0.0 0.0 copy-start.3
  0.7 0.0 copy-start.4
  0.7 0.0 copy-start.5
  0.7 0.0 copy-done.3
  0.7 0.6 copy-done.4
  1.3 0.0 copy-done.5
  1.3 0.0 copy-start
  1.3 1.0 %copy-done = bf16[1,4,128,440]{2,3,1,0:T(8,128)(2,1)S(1)} copy-done((bf16[1,4,128,440]{2,3,1,0:T(8,128)(2,1)S(1)}, bf16[1,4,128,440]{2,3,1,0:T(8,128)(2,1)}, u32[]{:S(2)}) %copy-start) | copy-done | bytes 450584
  2.4 0.0 copy-start.1
  2.4 0.9 %copy-done.1 = bf16[1,2,128,440]{2,3,1,0:T(8,128)(2,1)S(1)} copy-done((bf16[1,2,128,440]{2,3,1,0:T(8,128)(2,1)S(1)}, bf16[1,2,128,440]{2,3,1,0:T(8,128)(2,1)}, u32[]{:S(2)}) %copy-start.1) | copy-done | bytes 225304
  3.3 0.0 copy-start.2
  3.3 0.7 copy-done.2
  4.0 0.8 %shard_map.73 = bf16[3072,128]{1,0:T(8,128)(2,1)S(1)} custom-call(s32[1,1]{1,0:T(1,128)S(6)} %copy.8.count_ref, bf16[1,4,440,128]{3,2,1,0:T(8,128)(2,1)S(1)} %bitcast.15, bf16[1,2,440,128]{3,2,1,0:T(8,128)(2,1)S(1)} %bitcast.16, s32[1,1,128]{2,1,0:T(1,128)S(1)} %copy-done.4, s32[1,1,128]{2,1,0:T(1,128)S(1)} %copy-done.5, s32[1,4,440]{2,1,0:T(4,128)S(1)} %copy-done.2, ...), custom_call_target="tpu_custom_call" | custom-call | tf_op jit(solution)/shard_map/pallas_call | solution.py:192
  4.8 28.0 %all_to_all.15 = bf16[128,24,128]{2,1,0:T(8,128)(2,1)S(1)} all-to-all(bf16[128,24,128]{2,1,0:T(8,128)(2,1)S(1)} %bitcast.9), channel_id=1, replica_groups=mesh['x'=4,'y_hi'=2,'core'=2,'y_lo'=2,'z'=4] {'x','y_hi','core','y_lo','z'}, dimensions={0} | all-to-all | bytes 1572864 | tf_op jit(solution)/shard_map/all_to_all | solution.py:168
  32.8 3.7 %shard_map.74 = (f32[768,128]{1,0:T(8,128)S(1)}, f32[768,128]{1,0:T(8,128)S(1)}) custom-call(bf16[3072,128]{1,0:T(8,128)(2,1)S(1)} %bitcast.8), custom_call_target="tpu_custom_call" | custom-call | tf_op jit(solution)/shard_map/pallas_call | solution.py:209
  36.5 0.8 %collective-permute-start = (f32[768,128]{1,0:T(8,128)S(1)}, f32[768,128]{1,0:T(8,128)S(1)}, u32[]{:S(2)}, u32[]{:S(2)}) collective-permute-start(f32[768,128]{1,0:T(8,128)S(1)} %get-tuple-element.8), channel_id=1, source_target_pairs={{0,8},{8,0},{1,9},{9,1},{2,10},{10,2},{3,11},{11,3},{4,12},{12,4},... | collective-permute-start | bytes 1179656 | tf_op jit(solution)/shard_map/ppermute | solution.py:172
  37.3 1.3 %collective-permute-done.b_ref = f32[768,128]{1,0:T(8,128)S(1)} collective-permute-done((f32[768,128]{1,0:T(8,128)S(1)}, f32[768,128]{1,0:T(8,128)S(1)}, u32[]{:S(2)}, u32[]{:S(2)}) %collective-permute-start) | collective-permute-done | bytes 393248 | tf_op jit(solution)/shard_map/ppermute | solution.py:172
  38.7 15.1 %all_to_all.16 = f32[64,3,4,128]{3,2,1,0:T(4,128)S(1)} all-to-all(f32[64,3,4,128]{3,2,1,0:T(4,128)S(1)} %bitcast.14), channel_id=1, replica_groups=mesh['x'=4,'y_hi'=2,'core'=2,'y_lo'=2,'z'=4] {'x','y_hi','y_lo','z'}, dimensions={0} | all-to-all | bytes 786432 | tf_op jit(solution)/shard_map/all_to_all | solution.py:168
  53.8 0.1 shard_map.76
  53.9 14.6 %all_to_all.17 = f32[64,3,4,128]{3,2,1,0:T(4,128)S(1)} all-to-all(f32[64,3,4,128]{3,2,1,0:T(4,128)S(1)} %bitcast.11), channel_id=1, replica_groups=mesh['x'=4,'y_hi'=2,'core'=2,'y_lo'=2,'z'=4] {'x','y_hi','y_lo','z'}, dimensions={0} | all-to-all | bytes 786432 | tf_op jit(solution)/shard_map/all_to_all | solution.py:168
  68.5 3.2 %collective-permute-start.1 = (f32[768,128]{1,0:T(8,128)S(1)}, f32[768,128]{1,0:T(8,128)S(1)}, u32[]{:S(2)}, u32[]{:S(2)}) collective-permute-start(f32[768,128]{1,0:T(8,128)S(1)} %bitcast.12), channel_id=1, source_target_pairs={{0,8},{8,0},{1,9},{9,1},{2,10},{10,2},{3,11},{11,3},{4,12},{12,4},... | collective-permute-start | bytes 1179656 | tf_op jit(solution)/shard_map/ppermute | solution.py:172
  71.6 1.3 %collective-permute-done.1.given_ref = f32[768,128]{1,0:T(8,128)S(1)} collective-permute-done((f32[768,128]{1,0:T(8,128)S(1)}, f32[768,128]{1,0:T(8,128)S(1)}, u32[]{:S(2)}, u32[]{:S(2)}) %collective-permute-start.1) | collective-permute-done | bytes 393248 | tf_op jit(solution)/shard_map/ppermute | solution.py:172
  73.0 1.0 %shard_map.77 = f32[440,440]{1,0:T(8,128)} custom-call(f32[768,128]{1,0:T(8,128)S(1)} %bitcast.13, f32[768,128]{1,0:T(8,128)S(1)} %collective-permute-done.1.given_ref), custom_call_target="tpu_custom_call" | custom-call | tf_op jit(solution)/shard_map/pallas_call | solution.py:225
  (1 shorter events, 0.0 us)
Async XLA Ops:
  0.0 0.7 copy-start.3
  0.7 0.7 copy-start.4
  0.7 0.7 copy-start.5
  1.3 1.0 %copy-start = (bf16[1,4,128,440]{2,3,1,0:T(8,128)(2,1)S(1)}, bf16[1,4,128,440]{2,3,1,0:T(8,128)(2,1)}, u32[]{:S(2)}) copy-start(bf16[1,4,128,440]{2,3,1,0:T(8,128)(2,1)} %param.7) | copy-start | bytes 1351684
  2.4 0.9 %copy-start.1 = (bf16[1,2,128,440]{2,3,1,0:T(8,128)(2,1)S(1)}, bf16[1,2,128,440]{2,3,1,0:T(8,128)(2,1)}, u32[]{:S(2)}) copy-start(bf16[1,2,128,440]{2,3,1,0:T(8,128)(2,1)} %param.8) | copy-start | bytes 675844
  3.3 0.7 copy-start.2
  36.5 2.1 %collective-permute-start = (f32[768,128]{1,0:T(8,128)S(1)}, f32[768,128]{1,0:T(8,128)S(1)}, u32[]{:S(2)}, u32[]{:S(2)}) collective-permute-start(f32[768,128]{1,0:T(8,128)S(1)} %get-tuple-element.8), channel_id=1, source_target_pairs={{0,8},{8,0},{1,9},{9,1},{2,10},{10,2},{3,11},{11,3},{4,12},{12,4},... | collective-permute-start | bytes 1179656 | tf_op jit(solution)/shard_map/ppermute | solution.py:172
  68.5 4.5 %collective-permute-start.1 = (f32[768,128]{1,0:T(8,128)S(1)}, f32[768,128]{1,0:T(8,128)S(1)}, u32[]{:S(2)}, u32[]{:S(2)}) collective-permute-start(f32[768,128]{1,0:T(8,128)S(1)} %bitcast.12), channel_id=1, source_target_pairs={{0,8},{8,0},{1,9},{9,1},{2,10},{10,2},{3,11},{11,3},{4,12},{12,4},... | collective-permute-start | bytes 1179656 | tf_op jit(solution)/shard_map/ppermute | solution.py:172

commit v3 on v2

--- a/solution.py
+++ b/solution.py
@@ -26,24 +26,32 @@
     return lax.broadcasted_iota(jnp.int32, shape, len(shape) - 1)
 
 
-def send_kernel(count_ref, final_ref, initial_ref, pf_ref, pi_ref, mf_ref, mi_ref, out_ref, maps, wide):
+def send_kernel(counts, finals, initials, pairs_final, pairs_initial, maps_final, maps_initial, out_ref, *scratch):
+    count, blocks, pf, pi, mf, mi, maps, wide, arrived = scratch
+    small = [(counts, count), (pairs_final, pf), (pairs_initial, pi), (maps_final, mf), (maps_initial, mi)]
+    large = [(finals.at[0, j], blocks.at[j]) for j in range(4)] + [(initials.at[0, j], blocks.at[4 + j]) for j in range(2)]
+    copies = [pltpu.make_async_copy(a, b, arrived.at[n]) for n, (a, b) in enumerate(small + large)]
+    for copy in copies:
+        copy.start()
     maps[...] = jnp.full(maps.shape, -1, jnp.int32)
-    maps[0:4, 0:440] = mf_ref[0]
-    maps[4:6, 0:440] = mi_ref[0]
+    for copy in copies[: len(small)]:
+        copy.wait()
+    maps[0:4, 0:440] = mf[0]
+    maps[4:6, 0:440] = mi[0]
     slot = lane_index((1, LANES))
-    q = pf_ref[0]
-    s = pi_ref[0]
-    q_code = jnp.where(slot < count_ref[0, 0], (q & 3) * 8 + (q >> 2), DEAD).astype(jnp.float32)
-    s_code = ((s & 1) * LANES + (s >> 1) * 8).astype(jnp.float32)
+    q = pf[0]
+    s = pi[0]
+    q_code = jnp.where(slot < count[...], (q & 3) * 8 + (q >> 2), DEAD).astype(jnp.float32)
+    s_code = ((s & 1) * 16 + (s >> 1)).astype(jnp.float32)
     q_code = jnp.broadcast_to(q_code, (8, LANES))
     s_code = jnp.broadcast_to(s_code, (8, LANES))
     info = [pltpu.roll(q_code, 64, 1), q_code, pltpu.roll(s_code, 64, 1), s_code]
     upper = lane_index((LANES, LANES)) >= 64
     for j in range(6):
-        block = final_ref[0, j] if j < 4 else initial_ref[0, j - 4]
         stored = lax.broadcasted_iota(jnp.int32, (440, 512), 0)
         pick = jnp.where(stored == maps[j : j + 1, :], 1.0, 0.0).astype(jnp.bfloat16)
-        ordered = lax.dot_general(block, pick, (((0,), (0,)), ((), ())), preferred_element_type=jnp.float32)
+        copies[len(small) + j].wait()
+        ordered = lax.dot_general(blocks[j], pick, (((0,), (0,)), ((), ())), preferred_element_type=jnp.float32)
         for chunk in range(4):
             part = ordered[:, chunk * LANES : (chunk + 1) * LANES]
             if chunk == 3 and j < 4:
@@ -52,51 +60,56 @@
     out_ref[...] = wide[...].astype(jnp.bfloat16)
 
 
-def density_kernel(in_ref, keep_ref, give_ref, wide, pairs, final, initial, full):
+def density_kernel(in_ref, keep_ref, give_ref, wide, pairs, final, initial, met, full):
     wide[...] = in_ref[...].astype(jnp.float32)
 
     def rows(r):
         return wide[pl.ds(r, DEVICES, stride=MESSAGE), :]
 
     lower = lane_index((LANES, LANES)) < 64
-    codes = [
-        jnp.where(lower, pltpu.roll(rows(3 + 8 * k), 64, 1), rows(7 + 8 * k)).astype(jnp.int32) for k in range(2)
-    ]
-    pairs[0:LANES, :] = codes[0]
-    pairs[LANES:, :] = codes[1] + (lax.broadcasted_iota(jnp.int32, (LANES, LANES), 0) & 7)
-
-    for j in range(4):
+    for k in range(2):
+        pairs[k * LANES : (k + 1) * LANES, :] = jnp.where(lower, pltpu.roll(rows(3 + 8 * k), 64, 1), rows(7 + 8 * k))
+
+    for r in range(16):
         for chunk in range(4):
-            final[j * LANES : (j + 1) * LANES, chunk * LANES : (chunk + 1) * LANES] = rows(j * 4 + chunk).astype(jnp.bfloat16)
+            part = [wide[pl.ds(r * 8 * MESSAGE + j * 4 + chunk, 8, stride=MESSAGE), :] for j in range(4)]
+            final[r * 32 : (r + 1) * 32, chunk * LANES : (chunk + 1) * LANES] = jnp.concatenate(part, axis=0).astype(jnp.bfloat16)
     for j in range(2):
         for chunk in range(4):
             part = rows(FINAL_ROWS + j * 4 + chunk).astype(jnp.bfloat16)
             initial[j * LANES : (j + 1) * LANES, chunk * LANES : (chunk + 1) * LANES] = part
             initial[(2 + j) * LANES : (3 + j) * LANES, chunk * LANES : (chunk + 1) * LANES] = part
 
-    final_is = lax.broadcasted_iota(jnp.int32, (32, LANES), 0)
-    initial_is = lax.broadcasted_iota(jnp.int32, (256, LANES), 0)
-    for r in range(16):
-        q = pairs[r * 8 : r * 8 + 8, :]
-        s = pairs[LANES + r * 8 : LANES + r * 8 + 8, :]
-        left = jnp.concatenate([jnp.where(final_is == q[c : c + 1], 1.0, 0.0) for c in range(8)], axis=1)
-        right = jnp.concatenate([jnp.where(initial_is == s[c : c + 1], 1.0, 0.0) for c in range(8)], axis=1)
-        met = lax.dot_general(
-            left.astype(jnp.bfloat16),
-            right.astype(jnp.bfloat16),
-            (((1,), (1,)), ((), ())),
-            preferred_element_type=jnp.float32,
-        )
-        for j in range(4):
-            full[j * LANES + r * 8 : j * LANES + r * 8 + 8, 0:256] = met[j * 8 : (j + 1) * 8]
-
-    met = full[:, 0:256].astype(jnp.bfloat16)
-    across = (((0,), (0,)), ((), ()))
-    summed = lax.dot_general(met, final[...], across, preferred_element_type=jnp.float32)
+    code = lax.broadcasted_iota(jnp.int32, (32, LANES), 0).astype(jnp.float32)
+
+    def one_hot(slots):
+        return jnp.where(code == slots, 1.0, 0.0).astype(jnp.bfloat16)
+
+    for c in range(8):
+        for g in range(4):
+            cells = []
+            for d in range(g * 32 + c, g * 32 + 32, 8):
+                cells.append(
+                    lax.dot_general(
+                        one_hot(pairs[LANES + d : LANES + d + 1, :]),
+                        one_hot(pairs[d : d + 1, :]),
+                        (((1,), (1,)), ((), ())),
+                        preferred_element_type=jnp.float32,
+                    )
+                )
+            cells = jnp.concatenate(cells, axis=1)
+            for j in range(2):
+                met[pl.ds(g * 256 + j * LANES + c, 16, stride=8), :] = cells[j * 16 : (j + 1) * 16]
+
+    times = jnp.concatenate([met[g * 256 : (g + 1) * 256, :].astype(jnp.bfloat16) for g in range(4)], axis=1)
+    summed = jnp.dot(times, final[...], preferred_element_type=jnp.float32)
     high = summed.astype(jnp.bfloat16)
     low = (summed - high.astype(jnp.float32)).astype(jnp.bfloat16)
     full[...] = lax.dot_general(
-        jnp.concatenate([high, low], axis=0), initial[...], across, preferred_element_type=jnp.float32
+        jnp.concatenate([high, low], axis=0),
+        initial[...],
+        (((0,), (0,)), ((), ())),
+        preferred_element_type=jnp.float32,
     )
 
     lane = lane_index((8, LANES))
@@ -137,8 +150,11 @@
         out_ref[d * 24 : (d + 1) * 24, :] = twice
 
 
-def place_kernel(kept_ref, given_ref, out_ref):
+def place_kernel(kept_ref, given_ref, out_hbm, out_ref, sent):
     lane = lane_index((8, LANES))
+    copies = [
+        pltpu.make_async_copy(out_ref.at[n * 88 : (n + 1) * 88], out_hbm.at[n * 88 : (n + 1) * 88], sent.at[n]) for n in range(5)
+    ]
 
     def place(first, second):
         def tile(t):
@@ -158,10 +174,14 @@
                     piece = pltpu.roll(tile(STRIPS * 3 + k), (8 * k - TAIL) % LANES, 1)
                     strip = jnp.where((lane >= 8 * k) & (lane < 8 * k + 8), piece, strip)
             out_ref[e * 8 : (e + 1) * 8, 3 * LANES : 440] = strip[:, 0:TAIL]
+            if e % 11 == 10:
+                copies[e // 11].start()
 
     core = lax.axis_index("core")
     pl.when(core == 0)(lambda: place(kept_ref, given_ref))
     pl.when(core == 1)(lambda: place(given_ref, kept_ref))
+    for copy in copies:
+        copy.wait()
 
 
 def exchange(x, axes, shape):
@@ -174,7 +194,6 @@
 
 def shards(final_amp, initial_amp, pair_final, pair_initial, map_final, map_initial, counts):
     vmem = pl.BlockSpec(memory_space=pltpu.VMEM)
-    smem = pl.BlockSpec(memory_space=pltpu.SMEM)
     f32, bf16 = jnp.float32, jnp.bfloat16
     half = jax.ShapeDtypeStruct((CHIPS * SLICE, LANES), f32)
 
@@ -192,10 +211,20 @@
     messages = pl.pallas_call(
         send_kernel,
         out_shape=jax.ShapeDtypeStruct((DEVICES * MESSAGE, LANES), bf16),
-        in_specs=[smem] + [vmem] * 6,
+        in_specs=[pl.BlockSpec(memory_space=pltpu.HBM)] * 7,
         out_specs=vmem,
-        scratch_shapes=[pltpu.VMEM((8, 512), jnp.int32), pltpu.VMEM((DEVICES * MESSAGE, LANES), f32)],
-        compiler_params=PARAMS,
+        scratch_shapes=[
+            pltpu.VMEM((1, 1), jnp.int32),
+            pltpu.VMEM((6, 440, LANES), bf16),
+            pltpu.VMEM((1, 1, LANES), jnp.int32),
+            pltpu.VMEM((1, 1, LANES), jnp.int32),
+            pltpu.VMEM((1, 4, 440), jnp.int32),
+            pltpu.VMEM((1, 2, 440), jnp.int32),
+            pltpu.VMEM((8, 512), jnp.int32),
+            pltpu.VMEM((DEVICES * MESSAGE, LANES), f32),
+            pltpu.SemaphoreType.DMA((11,)),
+        ],
+        compiler_params=pltpu.CompilerParams(vmem_limit_bytes=60 * 1024 * 1024),
     )(
         counts,
         jnp.swapaxes(final_amp, 2, 3),
@@ -212,9 +241,10 @@
         1,
         [
             pltpu.VMEM((DEVICES * MESSAGE, LANES), f32),
-            pltpu.VMEM((2 * LANES, LANES), jnp.int32),
+            pltpu.VMEM((2 * LANES, LANES), f32),
             pltpu.VMEM((512, 512), bf16),
             pltpu.VMEM((512, 512), bf16),
+            pltpu.VMEM((4 * 256, LANES), f32),
             pltpu.VMEM((512, 512), f32),
         ],
     )(received)
@@ -222,7 +252,14 @@
     shares = exchange(share, ACROSS_CHIPS, (CHIPS, 3, 4, LANES))
     copies = call(sum_kernel, half, 1)(shares)
     slices = exchange(copies, ACROSS_CHIPS, (CHIPS, 3, 4, LANES))
-    return call(place_kernel, jax.ShapeDtypeStruct((440, 440), f32), 2)(slices, to_other_core(slices))
+    return pl.pallas_call(
+        place_kernel,
+        out_shape=jax.ShapeDtypeStruct((440, 440), f32),
+        in_specs=[vmem] * 2,
+        out_specs=pl.BlockSpec(memory_space=pltpu.HBM),
+        scratch_shapes=[pltpu.VMEM((440, 440), f32), pltpu.SemaphoreType.DMA((5,))],
+        compiler_params=PARAMS,
+    )(slices, to_other_core(slices))
 
 
 def solution(mesh):

time: 74.3 us -> 72.5 us (0.976)
  local copies, waits for them, and re-layouts: 3.3 us -> 0 us
  Pallas kernels: 5.63 us -> 7.01 us
    unnamed x12 -> x0, local copies, waits for them, and re-layouts: 3.3 us -> none
    pallas_call x1, Pallas kernels: 0.79 us -> 4.05 us  [shards(): pl.pallas_call(send_kernel, out_shape=jax.ShapeDtypeStruct((DEVICES * MES...]
    pallas_call x1, Pallas kernels: 3.71 us -> 1.89 us  [shards(): call(density_kernel, [half, half], 1, [pltpu.VMEM((DEVICES * MESSAGE, LAN...]
where the time goes in v3:
time: 72.5 us; the launch traced here: 72.3 us
  blocking collectives  57.9 us (80%)
  Pallas kernels  7.01 us (10%)
  starting transfers between devices  3.95 us (5%)
  waiting for transfers between devices  2.7 us (4%)
    all_to_all x3, blocking collectives, exchange(): lax.all_to_all(x.reshape(shape), axes, 0, 0, tiled=True).reshape(x.shape)  57.9 us
    pallas_call x1, Pallas kernels, shards(): pl.pallas_call(send_kernel, out_shape=jax.ShapeDtypeStruct((DEVICES * MES...  4.05 us
    ppermute x2, starting transfers between devices, to_other_core(): return lax.ppermute(x, 'core', [(0, 1), (1, 0)])  3.95 us
    ppermute x2, waiting for transfers between devices, to_other_core(): return lax.ppermute(x, 'core', [(0, 1), (1, 0)])  2.7 us
    pallas_call x1, Pallas kernels, shards(): call(density_kernel, [half, half], 1, [pltpu.VMEM((DEVICES * MESSAGE, LAN...  1.89 us
  transfers between devices with their start and end apart: 2, of which 2 were waited for; matrix products, arithmetic and copies ran while one was open for 0% of the time, Pallas kernels for 0%

profile of v3, /device:TPU:1, one launch (start us, length us, event | category | flops | bytes accessed | tf_op | source)
XLA Modules:
  0.0 72.3 jit_solution(6273910956808420607)
XLA Ops:
  0.7 4.0 %shard_map.73 = bf16[3072,128]{1,0:T(8,128)(2,1)} custom-call(s32[1,1]{1,0:T(1,128)S(6)} %copy.8.counts, bf16[1,4,440,128]{3,2,1,0:T(8,128)(2,1)} %bitcast.15, bf16[1,2,440,128]{3,2,1,0:T(8,128)(2,1)} %bitcast.16, s32[1,1,128]{2,1,0:T(1,128)} %pairs_final.1, s32[1,1,128]{2,1,0:T(1,128)} %pairs_initial.1, s32[1,4,440]{2,1,0:T(4,128)} %maps_final.1, ...), custom_call_target="tpu_custom_call" | custom-call | tf_op jit(solution)/shard_map/pallas_call | solution.py:211
  4.7 28.2 %all_to_all.15 = bf16[128,24,128]{2,1,0:T(8,128)(2,1)S(1)} all-to-all(bf16[128,24,128]{2,1,0:T(8,128)(2,1)} %bitcast.14), channel_id=1, replica_groups=mesh['x'=4,'y_hi'=2,'core'=2,'y_lo'=2,'z'=4] {'x','y_hi','core','y_lo','z'}, dimensions={0} | all-to-all | bytes 1572864 | tf_op jit(solution)/shard_map/all_to_all | solution.py:188
  33.0 1.9 %shard_map.74 = (f32[768,128]{1,0:T(8,128)S(1)}, f32[768,128]{1,0:T(8,128)S(1)}) custom-call(bf16[3072,128]{1,0:T(8,128)(2,1)S(1)} %bitcast.8), custom_call_target="tpu_custom_call" | custom-call | tf_op jit(solution)/shard_map/pallas_call | solution.py:238
  34.9 0.8 %collective-permute-start = (f32[768,128]{1,0:T(8,128)S(1)}, f32[768,128]{1,0:T(8,128)S(1)}, u32[]{:S(2)}, u32[]{:S(2)}) collective-permute-start(f32[768,128]{1,0:T(8,128)S(1)} %get-tuple-element.8), channel_id=1, source_target_pairs={{0,8},{8,0},{1,9},{9,1},{2,10},{10,2},{3,11},{11,3},{4,12},{12,4},... | collective-permute-start | bytes 1179656 | tf_op jit(solution)/shard_map/ppermute | solution.py:192
  35.6 1.3 %collective-permute-done.b_ref = f32[768,128]{1,0:T(8,128)S(1)} collective-permute-done((f32[768,128]{1,0:T(8,128)S(1)}, f32[768,128]{1,0:T(8,128)S(1)}, u32[]{:S(2)}, u32[]{:S(2)}) %collective-permute-start) | collective-permute-done | bytes 393248 | tf_op jit(solution)/shard_map/ppermute | solution.py:192
  37.0 15.1 %all_to_all.16 = f32[64,3,4,128]{3,2,1,0:T(4,128)S(1)} all-to-all(f32[64,3,4,128]{3,2,1,0:T(4,128)S(1)} %bitcast.13), channel_id=1, replica_groups=mesh['x'=4,'y_hi'=2,'core'=2,'y_lo'=2,'z'=4] {'x','y_hi','y_lo','z'}, dimensions={0} | all-to-all | bytes 786432 | tf_op jit(solution)/shard_map/all_to_all | solution.py:188
  52.1 0.1 shard_map.76
  52.2 14.6 %all_to_all.17 = f32[64,3,4,128]{3,2,1,0:T(4,128)S(1)} all-to-all(f32[64,3,4,128]{3,2,1,0:T(4,128)S(1)} %bitcast.10), channel_id=1, replica_groups=mesh['x'=4,'y_hi'=2,'core'=2,'y_lo'=2,'z'=4] {'x','y_hi','y_lo','z'}, dimensions={0} | all-to-all | bytes 786432 | tf_op jit(solution)/shard_map/all_to_all | solution.py:188
  66.8 3.2 %collective-permute-start.1 = (f32[768,128]{1,0:T(8,128)S(1)}, f32[768,128]{1,0:T(8,128)S(1)}, u32[]{:S(2)}, u32[]{:S(2)}) collective-permute-start(f32[768,128]{1,0:T(8,128)S(1)} %bitcast.11), channel_id=1, source_target_pairs={{0,8},{8,0},{1,9},{9,1},{2,10},{10,2},{3,11},{11,3},{4,12},{12,4},... | collective-permute-start | bytes 1179656 | tf_op jit(solution)/shard_map/ppermute | solution.py:192
  69.9 1.3 %collective-permute-done.1.given_ref = f32[768,128]{1,0:T(8,128)S(1)} collective-permute-done((f32[768,128]{1,0:T(8,128)S(1)}, f32[768,128]{1,0:T(8,128)S(1)}, u32[]{:S(2)}, u32[]{:S(2)}) %collective-permute-start.1) | collective-permute-done | bytes 393248 | tf_op jit(solution)/shard_map/ppermute | solution.py:192
  71.3 1.0 %shard_map.77 = f32[440,440]{1,0:T(8,128)} custom-call(f32[768,128]{1,0:T(8,128)S(1)} %bitcast.12, f32[768,128]{1,0:T(8,128)S(1)} %collective-permute-done.1.given_ref), custom_call_target="tpu_custom_call" | custom-call | tf_op jit(solution)/shard_map/pallas_call | solution.py:255
  (1 shorter events, 0.0 us)
Async XLA Ops:
  34.9 2.1 %collective-permute-start = (f32[768,128]{1,0:T(8,128)S(1)}, f32[768,128]{1,0:T(8,128)S(1)}, u32[]{:S(2)}, u32[]{:S(2)}) collective-permute-start(f32[768,128]{1,0:T(8,128)S(1)} %get-tuple-element.8), channel_id=1, source_target_pairs={{0,8},{8,0},{1,9},{9,1},{2,10},{10,2},{3,11},{11,3},{4,12},{12,4},... | collective-permute-start | bytes 1179656 | tf_op jit(solution)/shard_map/ppermute | solution.py:192
  66.8 4.5 %collective-permute-start.1 = (f32[768,128]{1,0:T(8,128)S(1)}, f32[768,128]{1,0:T(8,128)S(1)}, u32[]{:S(2)}, u32[]{:S(2)}) collective-permute-start(f32[768,128]{1,0:T(8,128)S(1)} %bitcast.11), channel_id=1, source_target_pairs={{0,8},{8,0},{1,9},{9,1},{2,10},{10,2},{3,11},{11,3},{4,12},{12,4},... | collective-permute-start | bytes 1179656 | tf_op jit(solution)/shard_map/ppermute | solution.py:192

commit v4 on v3

--- a/solution.py
+++ b/solution.py
@@ -27,21 +27,27 @@
 
 
 def send_kernel(counts, finals, initials, pairs_final, pairs_initial, maps_final, maps_initial, out_ref, *scratch):
-    count, blocks, pf, pi, mf, mi, maps, wide, arrived = scratch
-    small = [(counts, count), (pairs_final, pf), (pairs_initial, pi), (maps_final, mf), (maps_initial, mi)]
-    large = [(finals.at[0, j], blocks.at[j]) for j in range(4)] + [(initials.at[0, j], blocks.at[4 + j]) for j in range(2)]
-    copies = [pltpu.make_async_copy(a, b, arrived.at[n]) for n, (a, b) in enumerate(small + large)]
+    blocks, pf, pi, mf, mi, maps, wide, arrived = scratch
+    pairs = [
+        (finals.at[0], blocks.at[0:4]),
+        (initials.at[0], blocks.at[4:6]),
+        (maps_final, mf),
+        (maps_initial, mi),
+        (pairs_final, pf),
+        (pairs_initial, pi),
+    ]
+    copies = [pltpu.make_async_copy(there, here, arrived.at[n]) for n, (there, here) in enumerate(pairs)]
     for copy in copies:
         copy.start()
     maps[...] = jnp.full(maps.shape, -1, jnp.int32)
-    for copy in copies[: len(small)]:
+    for copy in copies:
         copy.wait()
     maps[0:4, 0:440] = mf[0]
     maps[4:6, 0:440] = mi[0]
     slot = lane_index((1, LANES))
     q = pf[0]
     s = pi[0]
-    q_code = jnp.where(slot < count[...], (q & 3) * 8 + (q >> 2), DEAD).astype(jnp.float32)
+    q_code = jnp.where(slot < counts[0, 0], (q & 3) * 8 + (q >> 2), DEAD).astype(jnp.float32)
     s_code = ((s & 1) * 16 + (s >> 1)).astype(jnp.float32)
     q_code = jnp.broadcast_to(q_code, (8, LANES))
     s_code = jnp.broadcast_to(s_code, (8, LANES))
@@ -50,7 +56,6 @@
     for j in range(6):
         stored = lax.broadcasted_iota(jnp.int32, (440, 512), 0)
         pick = jnp.where(stored == maps[j : j + 1, :], 1.0, 0.0).astype(jnp.bfloat16)
-        copies[len(small) + j].wait()
         ordered = lax.dot_general(blocks[j], pick, (((0,), (0,)), ((), ())), preferred_element_type=jnp.float32)
         for chunk in range(4):
             part = ordered[:, chunk * LANES : (chunk + 1) * LANES]
@@ -211,10 +216,9 @@
     messages = pl.pallas_call(
         send_kernel,
         out_shape=jax.ShapeDtypeStruct((DEVICES * MESSAGE, LANES), bf16),
-        in_specs=[pl.BlockSpec(memory_space=pltpu.HBM)] * 7,
+        in_specs=[pl.BlockSpec(memory_space=pltpu.SMEM)] + [pl.BlockSpec(memory_space=pltpu.HBM)] * 6,
         out_specs=vmem,
         scratch_shapes=[
-            pltpu.VMEM((1, 1), jnp.int32),
             pltpu.VMEM((6, 440, LANES), bf16),
             pltpu.VMEM((1, 1, LANES), jnp.int32),
             pltpu.VMEM((1, 1, LANES), jnp.int32),
@@ -222,17 +226,22 @@
             pltpu.VMEM((1, 2, 440), jnp.int32),
             pltpu.VMEM((8, 512), jnp.int32),
             pltpu.VMEM((DEVICES * MESSAGE, LANES), f32),
-            pltpu.SemaphoreType.DMA((11,)),
+            pltpu.SemaphoreType.DMA((6,)),
         ],
-        compiler_params=pltpu.CompilerParams(vmem_limit_bytes=60 * 1024 * 1024),
+        compiler_params=PARAMS,
     )(
         counts,
-        jnp.swapaxes(final_amp, 2, 3),
-        jnp.swapaxes(initial_amp, 2, 3),
-        pair_final,
-        pair_initial,
-        map_final,
-        map_initial,
+        *(
+            pltpu.with_memory_space_constraint(x, pltpu.HBM)
+            for x in (
+                jnp.swapaxes(final_amp, 2, 3),
+                jnp.swapaxes(initial_amp, 2, 3),
+                pair_final,
+                pair_initial,
+                map_final,
+                map_initial,
+            )
+        )
     )
     received = exchange(messages, ALL, (DEVICES, MESSAGE, LANES))
     keep, give = call(

time: 72.5 us -> 70.1 us (0.967)
  Pallas kernels: 7.01 us -> 4.88 us
    pallas_call x1, Pallas kernels: 4.05 us -> 1.92 us  [shards(): pl.pallas_call(send_kernel, out_shape=jax.ShapeDtypeStruct((DEVICES * MES...]
where the time goes in v4:
time: 70.1 us; the launch traced here: 69.9 us
  blocking collectives  57.7 us (82%)
  Pallas kernels  4.88 us (7%)
  starting transfers between devices  3.94 us (6%)
  waiting for transfers between devices  2.7 us (4%)
    all_to_all x3, blocking collectives, exchange(): lax.all_to_all(x.reshape(shape), axes, 0, 0, tiled=True).reshape(x.shape)  57.7 us
    ppermute x2, starting transfers between devices, to_other_core(): return lax.ppermute(x, 'core', [(0, 1), (1, 0)])  3.94 us
    ppermute x2, waiting for transfers between devices, to_other_core(): return lax.ppermute(x, 'core', [(0, 1), (1, 0)])  2.7 us
    pallas_call x1, Pallas kernels, shards(): pl.pallas_call(send_kernel, out_shape=jax.ShapeDtypeStruct((DEVICES * MES...  1.92 us
    pallas_call x1, Pallas kernels, shards(): call(density_kernel, [half, half], 1, [pltpu.VMEM((DEVICES * MESSAGE, LAN...  1.89 us
  transfers between devices with their start and end apart: 2, of which 2 were waited for; matrix products, arithmetic and copies ran while one was open for 0% of the time, Pallas kernels for 0%

profile of v4, /device:TPU:1, one launch (start us, length us, event | category | flops | bytes accessed | tf_op | source)
XLA Modules:
  0.0 69.9 jit_solution(8893096097968663907)
XLA Ops:
  0.7 1.9 %shard_map.73 = bf16[3072,128]{1,0:T(8,128)(2,1)S(1)} custom-call(s32[1,1]{1,0:T(1,128)S(6)} %copy.8.counts, bf16[1,4,440,128]{3,2,1,0:T(8,128)(2,1)} %bitcast.15, bf16[1,2,440,128]{3,2,1,0:T(8,128)(2,1)} %bitcast.16, s32[1,1,128]{2,1,0:T(1,128)} %pairs_final.1, s32[1,1,128]{2,1,0:T(1,128)} %pairs_initial.1, s32[1,4,440]{2,1,0:T(4,128)} %maps_final.1, ...), custom_call_target="tpu_custom_call" | custom-call | tf_op jit(solution)/shard_map/pallas_call | solution.py:216
  2.6 28.0 %all_to_all.15 = bf16[128,24,128]{2,1,0:T(8,128)(2,1)S(1)} all-to-all(bf16[128,24,128]{2,1,0:T(8,128)(2,1)S(1)} %bitcast.9), channel_id=1, replica_groups=mesh['x'=4,'y_hi'=2,'core'=2,'y_lo'=2,'z'=4] {'x','y_hi','core','y_lo','z'}, dimensions={0} | all-to-all | bytes 1572864 | tf_op jit(solution)/shard_map/all_to_all | solution.py:193
  30.6 1.9 %shard_map.74 = (f32[768,128]{1,0:T(8,128)S(1)}, f32[768,128]{1,0:T(8,128)S(1)}) custom-call(bf16[3072,128]{1,0:T(8,128)(2,1)S(1)} %bitcast.8), custom_call_target="tpu_custom_call" | custom-call | tf_op jit(solution)/shard_map/pallas_call | solution.py:247
  32.5 0.8 %collective-permute-start = (f32[768,128]{1,0:T(8,128)S(1)}, f32[768,128]{1,0:T(8,128)S(1)}, u32[]{:S(2)}, u32[]{:S(2)}) collective-permute-start(f32[768,128]{1,0:T(8,128)S(1)} %get-tuple-element.8), channel_id=1, source_target_pairs={{0,8},{8,0},{1,9},{9,1},{2,10},{10,2},{3,11},{11,3},{4,12},{12,4},... | collective-permute-start | bytes 1179656 | tf_op jit(solution)/shard_map/ppermute | solution.py:197
  33.3 1.3 %collective-permute-done.b_ref = f32[768,128]{1,0:T(8,128)S(1)} collective-permute-done((f32[768,128]{1,0:T(8,128)S(1)}, f32[768,128]{1,0:T(8,128)S(1)}, u32[]{:S(2)}, u32[]{:S(2)}) %collective-permute-start) | collective-permute-done | bytes 393248 | tf_op jit(solution)/shard_map/ppermute | solution.py:197
  34.7 15.1 %all_to_all.16 = f32[64,3,4,128]{3,2,1,0:T(4,128)S(1)} all-to-all(f32[64,3,4,128]{3,2,1,0:T(4,128)S(1)} %bitcast.14), channel_id=1, replica_groups=mesh['x'=4,'y_hi'=2,'core'=2,'y_lo'=2,'z'=4] {'x','y_hi','y_lo','z'}, dimensions={0} | all-to-all | bytes 786432 | tf_op jit(solution)/shard_map/all_to_all | solution.py:193
  49.8 0.1 shard_map.76
  49.8 14.6 %all_to_all.17 = f32[64,3,4,128]{3,2,1,0:T(4,128)S(1)} all-to-all(f32[64,3,4,128]{3,2,1,0:T(4,128)S(1)} %bitcast.11), channel_id=1, replica_groups=mesh['x'=4,'y_hi'=2,'core'=2,'y_lo'=2,'z'=4] {'x','y_hi','y_lo','z'}, dimensions={0} | all-to-all | bytes 786432 | tf_op jit(solution)/shard_map/all_to_all | solution.py:193
  64.4 3.2 %collective-permute-start.1 = (f32[768,128]{1,0:T(8,128)S(1)}, f32[768,128]{1,0:T(8,128)S(1)}, u32[]{:S(2)}, u32[]{:S(2)}) collective-permute-start(f32[768,128]{1,0:T(8,128)S(1)} %bitcast.12), channel_id=1, source_target_pairs={{0,8},{8,0},{1,9},{9,1},{2,10},{10,2},{3,11},{11,3},{4,12},{12,4},... | collective-permute-start | bytes 1179656 | tf_op jit(solution)/shard_map/ppermute | solution.py:197
  67.6 1.3 %collective-permute-done.1.given_ref = f32[768,128]{1,0:T(8,128)S(1)} collective-permute-done((f32[768,128]{1,0:T(8,128)S(1)}, f32[768,128]{1,0:T(8,128)S(1)}, u32[]{:S(2)}, u32[]{:S(2)}) %collective-permute-start.1) | collective-permute-done | bytes 393248 | tf_op jit(solution)/shard_map/ppermute | solution.py:197
  68.9 1.0 %shard_map.77 = f32[440,440]{1,0:T(8,128)} custom-call(f32[768,128]{1,0:T(8,128)S(1)} %bitcast.13, f32[768,128]{1,0:T(8,128)S(1)} %collective-permute-done.1.given_ref), custom_call_target="tpu_custom_call" | custom-call | tf_op jit(solution)/shard_map/pallas_call | solution.py:264
  (1 shorter events, 0.0 us)
Async XLA Ops:
  32.5 2.1 %collective-permute-start = (f32[768,128]{1,0:T(8,128)S(1)}, f32[768,128]{1,0:T(8,128)S(1)}, u32[]{:S(2)}, u32[]{:S(2)}) collective-permute-start(f32[768,128]{1,0:T(8,128)S(1)} %get-tuple-element.8), channel_id=1, source_target_pairs={{0,8},{8,0},{1,9},{9,1},{2,10},{10,2},{3,11},{11,3},{4,12},{12,4},... | collective-permute-start | bytes 1179656 | tf_op jit(solution)/shard_map/ppermute | solution.py:197
  64.4 4.5 %collective-permute-start.1 = (f32[768,128]{1,0:T(8,128)S(1)}, f32[768,128]{1,0:T(8,128)S(1)}, u32[]{:S(2)}, u32[]{:S(2)}) collective-permute-start(f32[768,128]{1,0:T(8,128)S(1)} %bitcast.12), channel_id=1, source_target_pairs={{0,8},{8,0},{1,9},{9,1},{2,10},{10,2},{3,11},{11,3},{4,12},{12,4},... | collective-permute-start | bytes 1179656 | tf_op jit(solution)/shard_map/ppermute | solution.py:197

commit v5 on v4

--- a/solution.py
+++ b/solution.py
@@ -12,9 +12,9 @@
 FINAL_ROWS = 16
 MESSAGE = 24
 SLICE = 12
-TILES = 192
-STRIPS = 55
-HALF = 27
+HALF_ORB = 220
+FULL_TILES = 27
+PACKED = 13
 TAIL = 56
 DEAD = 64
 ALL = ("x", "y_hi", "core", "y_lo", "z")
@@ -42,7 +42,8 @@
     maps[...] = jnp.full(maps.shape, -1, jnp.int32)
     for copy in copies:
         copy.wait()
-    maps[0:4, 0:440] = mf[0]
+    maps[0:4, 0:HALF_ORB] = mf[0, :, 0:HALF_ORB]
+    maps[0:4, 256 : 256 + HALF_ORB] = mf[0, :, HALF_ORB:440]
     maps[4:6, 0:440] = mi[0]
     slot = lane_index((1, LANES))
     q = pf[0]
@@ -51,39 +52,49 @@
     s_code = ((s & 1) * 16 + (s >> 1)).astype(jnp.float32)
     q_code = jnp.broadcast_to(q_code, (8, LANES))
     s_code = jnp.broadcast_to(s_code, (8, LANES))
-    info = [pltpu.roll(q_code, 64, 1), q_code, pltpu.roll(s_code, 64, 1), s_code]
-    upper = lane_index((LANES, LANES)) >= 64
+    info = [pltpu.roll(code, (96 - 32 * m) % LANES, 1) for code in (q_code, s_code) for m in range(4)]
+    last = lane_index((8, LANES)) >= 96
     for j in range(6):
         stored = lax.broadcasted_iota(jnp.int32, (440, 512), 0)
         pick = jnp.where(stored == maps[j : j + 1, :], 1.0, 0.0).astype(jnp.bfloat16)
         ordered = lax.dot_general(blocks[j], pick, (((0,), (0,)), ((), ())), preferred_element_type=jnp.float32)
         for chunk in range(4):
             part = ordered[:, chunk * LANES : (chunk + 1) * LANES]
-            if chunk == 3 and j < 4:
-                part = jnp.where(upper, jnp.broadcast_to(info[j][0:1], (LANES, LANES)), part)
-            wide[pl.ds(j * 4 + chunk, DEVICES, stride=MESSAGE), :] = part
+            if j >= 4:
+                wide[pl.ds(j * 4 + chunk, DEVICES, stride=MESSAGE), :] = part
+                continue
+            core, place = chunk // 2, chunk % 2
+            for group in range(16):
+                other = core ^ (group % 2)
+                rows = part[group * 8 : (group + 1) * 8]
+                if place == 1:
+                    rows = jnp.where(last, info[j * 2 + other], rows)
+                first = (group // 2 * 2 + core) * 8 * MESSAGE + j * 4 + other * 2 + place
+                wide[pl.ds(first, 8, stride=MESSAGE), :] = rows
     out_ref[...] = wide[...].astype(jnp.bfloat16)
 
 
-def density_kernel(in_ref, keep_ref, give_ref, wide, pairs, final, initial, met, full):
+def widen_kernel(in_ref, wide, initial):
     wide[...] = in_ref[...].astype(jnp.float32)
-
-    def rows(r):
-        return wide[pl.ds(r, DEVICES, stride=MESSAGE), :]
-
-    lower = lane_index((LANES, LANES)) < 64
+    for j in range(2):
+        for chunk in range(4):
+            part = wide[pl.ds(FINAL_ROWS + j * 4 + chunk, DEVICES, stride=MESSAGE), :].astype(jnp.bfloat16)
+            initial[j * LANES : (j + 1) * LANES, chunk * LANES : (chunk + 1) * LANES] = part
+
+
+def times_kernel(wide, out_ref, pairs, final, met):
+    quarter = lane_index((LANES, LANES)) // 32
     for k in range(2):
-        pairs[k * LANES : (k + 1) * LANES, :] = jnp.where(lower, pltpu.roll(rows(3 + 8 * k), 64, 1), rows(7 + 8 * k))
+        codes = jnp.zeros((LANES, LANES), jnp.float32)
+        for m in range(4):
+            piece = wide[pl.ds(1 + 2 * m + 8 * k, DEVICES, stride=MESSAGE), :]
+            codes = jnp.where(quarter == m, pltpu.roll(piece, (32 * m - 96) % LANES, 1), codes)
+        pairs[k * LANES : (k + 1) * LANES, :] = codes
 
     for r in range(16):
         for chunk in range(4):
             part = [wide[pl.ds(r * 8 * MESSAGE + j * 4 + chunk, 8, stride=MESSAGE), :] for j in range(4)]
             final[r * 32 : (r + 1) * 32, chunk * LANES : (chunk + 1) * LANES] = jnp.concatenate(part, axis=0).astype(jnp.bfloat16)
-    for j in range(2):
-        for chunk in range(4):
-            part = rows(FINAL_ROWS + j * 4 + chunk).astype(jnp.bfloat16)
-            initial[j * LANES : (j + 1) * LANES, chunk * LANES : (chunk + 1) * LANES] = part
-            initial[(2 + j) * LANES : (3 + j) * LANES, chunk * LANES : (chunk + 1) * LANES] = part
 
     code = lax.broadcasted_iota(jnp.int32, (32, LANES), 0).astype(jnp.float32)
 
@@ -110,39 +121,40 @@
     summed = jnp.dot(times, final[...], preferred_element_type=jnp.float32)
     high = summed.astype(jnp.bfloat16)
     low = (summed - high.astype(jnp.float32)).astype(jnp.bfloat16)
+    for other in range(2):
+        columns = slice(other * 256, (other + 1) * 256)
+        out_ref[other * 512 : other * 512 + 256, :] = high[:, columns]
+        out_ref[other * 512 + 256 : other * 512 + 512, :] = low[:, columns]
+
+
+def density_kernel(summed_ref, own_ref, other_ref, out_ref, full):
+    own, other = own_ref[...], other_ref[...]
     full[...] = lax.dot_general(
-        jnp.concatenate([high, low], axis=0),
-        initial[...],
+        summed_ref[...],
+        jnp.concatenate([own, own, other, other], axis=0),
         (((0,), (0,)), ((), ())),
         preferred_element_type=jnp.float32,
     )
-
     lane = lane_index((8, LANES))
+    upper = lax.broadcasted_iota(jnp.int32, (8, LANES), 0) < 4
 
     def tile(e, chunk):
         return full[e * 8 : (e + 1) * 8, chunk * LANES : (chunk + 1) * LANES]
 
-    def packed(t):
-        if t < STRIPS * 3:
-            return tile(t // 3, t % 3)
-        e = t - STRIPS * 3
-        two = jnp.where(lane < 64, tile(e, 3), pltpu.roll(tile(e + HALF, 3), 64, 1))
-        if e < 7:
-            two = jnp.where((lane >= TAIL) & (lane < 64), pltpu.roll(tile(STRIPS - 1, 3), TAIL - 8 * e, 1), two)
-        return two
-
-    def split(first, second):
-        for t in range(TILES // 2):
-            first[t * 8 : (t + 1) * 8, :] = packed(t)
-            second[t * 8 : (t + 1) * 8, :] = packed(t + TILES // 2)
-
-    core = lax.axis_index("core")
-    pl.when(core == 0)(lambda: split(keep_ref, give_ref))
-    pl.when(core == 1)(lambda: split(give_ref, keep_ref))
-
-
-def add_kernel(a_ref, b_ref, out_ref):
-    out_ref[...] = a_ref[...] + b_ref[...]
+    def put(t, value):
+        out_ref[t * 8 : (t + 1) * 8, :] = value
+
+    for e in range(FULL_TILES):
+        for chunk in range(3):
+            put(e * 3 + chunk, tile(e, chunk))
+    for u in range(PACKED):
+        two = jnp.where(lane < 64, tile(u, 3), pltpu.roll(tile(u + PACKED, 3), 64, 1))
+        if u < 7:
+            two = jnp.where((lane >= TAIL) & (lane < 64), pltpu.roll(tile(2 * PACKED, 3), TAIL - 8 * u, 1), two)
+        put(FULL_TILES * 3 + u, two)
+    for n in range(2):
+        two = jnp.where(upper, tile(FULL_TILES, 2 * n), pltpu.roll(tile(FULL_TILES, 2 * n + 1), 4, 0))
+        put(FULL_TILES * 3 + PACKED + n, two)
 
 
 def sum_kernel(in_ref, out_ref):
@@ -157,28 +169,42 @@
 
 def place_kernel(kept_ref, given_ref, out_hbm, out_ref, sent):
     lane = lane_index((8, LANES))
+    upper = lax.broadcasted_iota(jnp.int32, (8, LANES), 0) < 4
     copies = [
         pltpu.make_async_copy(out_ref.at[n * 88 : (n + 1) * 88], out_hbm.at[n * 88 : (n + 1) * 88], sent.at[n]) for n in range(5)
     ]
 
+    def tiles(half, e):
+        def got(t):
+            return half[t * 8 : (t + 1) * 8, :]
+
+        packed = FULL_TILES * 3
+        if e == FULL_TILES:
+            rest = [got(packed + PACKED), got(packed + PACKED + 1)]
+            return [rest[0], pltpu.roll(rest[0], 4, 0), rest[1], pltpu.roll(rest[1], 4, 0)]
+        if e < PACKED:
+            strip = got(packed + e)
+        elif e < 2 * PACKED:
+            strip = pltpu.roll(got(packed + e - PACKED), 64, 1)
+        else:
+            strip = jnp.zeros((8, LANES), jnp.float32)
+            for k in range(7):
+                piece = pltpu.roll(got(packed + k), (8 * k - TAIL) % LANES, 1)
+                strip = jnp.where((lane >= 8 * k) & (lane < 8 * k + 8), piece, strip)
+        return [got(e * 3), got(e * 3 + 1), got(e * 3 + 2), strip]
+
     def place(first, second):
-        def tile(t):
-            half, t = (first, t) if t < TILES // 2 else (second, t - TILES // 2)
-            return half[t * 8 : (t + 1) * 8, :]
-
-        for e in range(STRIPS):
+        below = None
+        for e in range(55):
+            if e < FULL_TILES:
+                row = tiles(first, e)
+            else:
+                above = tiles(first, e) if e == FULL_TILES else below
+                below = [pltpu.roll(x, 4, 0) for x in tiles(second, e - FULL_TILES)]
+                row = [jnp.where(upper, x, y) for x, y in zip(above, below)]
             for chunk in range(3):
-                out_ref[e * 8 : (e + 1) * 8, chunk * LANES : (chunk + 1) * LANES] = tile(e * 3 + chunk)
-            if e < HALF:
-                strip = tile(STRIPS * 3 + e)
-            elif e < STRIPS - 1:
-                strip = pltpu.roll(tile(STRIPS * 3 + e - HALF), 64, 1)
-            else:
-                strip = jnp.zeros((8, LANES), jnp.float32)
-                for k in range(7):
-                    piece = pltpu.roll(tile(STRIPS * 3 + k), (8 * k - TAIL) % LANES, 1)
-                    strip = jnp.where((lane >= 8 * k) & (lane < 8 * k + 8), piece, strip)
-            out_ref[e * 8 : (e + 1) * 8, 3 * LANES : 440] = strip[:, 0:TAIL]
+                out_ref[e * 8 : (e + 1) * 8, chunk * LANES : (chunk + 1) * LANES] = row[chunk]
+            out_ref[e * 8 : (e + 1) * 8, 3 * LANES : 440] = row[3][:, 0:TAIL]
             if e % 11 == 10:
                 copies[e // 11].start()
 
@@ -202,7 +228,7 @@
     f32, bf16 = jnp.float32, jnp.bfloat16
     half = jax.ShapeDtypeStruct((CHIPS * SLICE, LANES), f32)
 
-    def call(kernel, out_shape, n, scratch=()):
+    def call(kernel, out_shape, n, scratch=(), cost=None):
         several = isinstance(out_shape, list)
         return pl.pallas_call(
             kernel,
@@ -210,6 +236,7 @@
             in_specs=[vmem] * n,
             out_specs=[vmem] * len(out_shape) if several else vmem,
             scratch_shapes=list(scratch),
+            cost_estimate=cost,
             compiler_params=PARAMS,
         )
 
@@ -244,20 +271,24 @@
         )
     )
     received = exchange(messages, ALL, (DEVICES, MESSAGE, LANES))
-    keep, give = call(
-        density_kernel,
-        [half, half],
+    wide, own = call(
+        widen_kernel,
+        [jax.ShapeDtypeStruct((DEVICES * MESSAGE, LANES), f32), jax.ShapeDtypeStruct((256, 512), bf16)],
+        1,
+    )(received)
+    other = to_other_core(own)
+    summed = call(
+        times_kernel,
+        jax.ShapeDtypeStruct((1024, 256), bf16),
         1,
         [
-            pltpu.VMEM((DEVICES * MESSAGE, LANES), f32),
             pltpu.VMEM((2 * LANES, LANES), f32),
             pltpu.VMEM((512, 512), bf16),
-            pltpu.VMEM((512, 512), bf16),
             pltpu.VMEM((4 * 256, LANES), f32),
-            pltpu.VMEM((512, 512), f32),
         ],
-    )(received)
-    share = call(add_kernel, half, 2)(keep, to_other_core(give))
+        pl.CostEstimate(flops=10**9, bytes_accessed=8 * 10**6, transcendentals=0),
+    )(wide)
+    share = call(density_kernel, half, 3, [pltpu.VMEM((256, 512), f32)])(summed, own, other)
     shares = exchange(share, ACROSS_CHIPS, (CHIPS, 3, 4, LANES))
     copies = call(sum_kernel, half, 1)(shares)
     slices = exchange(copies, ACROSS_CHIPS, (CHIPS, 3, 4, LANES))

time: 70.1 us -> 68.9 us (0.983)
  waiting for transfers between devices: 2.7 us -> 1.35 us
    ppermute x2, waiting for transfers between devices: 2.7 us -> 1.35 us  [to_other_core(): return lax.ppermute(x, 'core', [(0, 1), (1, 0)])]
    pallas_call x2 -> x3, Pallas kernels: 1.94 us -> 1.98 us  [the longest x1 1.25 us: shards(): call(times_kernel, jax.ShapeDtypeStruct((1024, 256), bf16), 1, [pltpu.VME...]
  transfers between devices with their start and end apart: 2 -> 2, of which waited for: 2 -> 1; matrix products, arithmetic and copies ran while one was open for 0% -> 0% of each run, Pallas kernels for 0% -> 2%
where the time goes in v5:
time: 68.9 us; the launch traced here: 68.7 us
  blocking collectives  57.8 us (84%)
  Pallas kernels  4.98 us (7%)
  starting transfers between devices  3.85 us (6%)
  waiting for transfers between devices  1.35 us (2%)
  between operations  0.69 us (1%)
    all_to_all x3, blocking collectives, exchange(): lax.all_to_all(x.reshape(shape), axes, 0, 0, tiled=True).reshape(x.shape)  57.8 us
    ppermute x2, starting transfers between devices, to_other_core(): return lax.ppermute(x, 'core', [(0, 1), (1, 0)])  3.85 us
    pallas_call x1, Pallas kernels, shards(): pl.pallas_call(send_kernel, out_shape=jax.ShapeDtypeStruct((DEVICES * MES...  1.95 us
  transfers between devices with their start and end apart: 2, of which 1 were waited for; matrix products, arithmetic and copies ran while one was open for 0% of the time, Pallas kernels for 2%

profile of v5, /device:TPU:1, one launch (start us, length us, event | category | flops | bytes accessed | tf_op | source)
XLA Modules:
  0.0 68.7 jit_solution(147898399634280467)
XLA Ops:
  0.7 2.0 %shard_map.73 = bf16[3072,128]{1,0:T(8,128)(2,1)S(1)} custom-call(s32[1,1]{1,0:T(1,128)S(6)} %copy.8.counts, bf16[1,4,440,128]{3,2,1,0:T(8,128)(2,1)} %bitcast.15, bf16[1,2,440,128]{3,2,1,0:T(8,128)(2,1)} %bitcast.16, s32[1,1,128]{2,1,0:T(1,128)} %pairs_final.1, s32[1,1,128]{2,1,0:T(1,128)} %pairs_initial.1, s32[1,4,440]{2,1,0:T(4,128)} %maps_final.1, ...), custom_call_target="tpu_custom_call" | custom-call | tf_op jit(solution)/shard_map/pallas_call | solution.py:243
  2.6 28.0 %all_to_all.15 = bf16[128,24,128]{2,1,0:T(8,128)(2,1)S(1)} all-to-all(bf16[128,24,128]{2,1,0:T(8,128)(2,1)S(1)} %bitcast.9), channel_id=1, replica_groups=mesh['x'=4,'y_hi'=2,'core'=2,'y_lo'=2,'z'=4] {'x','y_hi','core','y_lo','z'}, dimensions={0} | all-to-all | bytes 1572864 | tf_op jit(solution)/shard_map/all_to_all | solution.py:219
  30.7 0.2 shard_map.74
  30.9 0.8 %collective-permute-start = (bf16[256,512]{1,0:T(8,128)(2,1)S(1)}, bf16[256,512]{1,0:T(8,128)(2,1)S(1)}, u32[]{:S(2)}, u32[]{:S(2)}) collective-permute-start(bf16[256,512]{1,0:T(8,128)(2,1)S(1)} %get-tuple-element.8.own_ref), channel_id=1, source_target_pairs={{0,8},{8,0},{1,9},{9,1},{2,10},{10,2},{3,11},{11,3},{4,12},{12,4},... | collective-permute-start | bytes 786440 | tf_op jit(solution)/shard_map/ppermute | solution.py:223
  31.7 1.2 %shard_map.75.summed_ref = bf16[1024,256]{1,0:T(8,128)(2,1)S(1)} custom-call(f32[3072,128]{1,0:T(8,128)S(1)} %get-tuple-element.7.wide), custom_call_target="tpu_custom_call" | custom-call | flops 1000000000 | bytes 8000000 | tf_op jit(solution)/shard_map/pallas_call | solution.py:280
  32.9 0.0 collective-permute-done.other_ref
  32.9 0.5 shard_map.76
  33.5 15.0 %all_to_all.16 = f32[64,3,4,128]{3,2,1,0:T(4,128)S(1)} all-to-all(f32[64,3,4,128]{3,2,1,0:T(4,128)S(1)} %bitcast.14), channel_id=1, replica_groups=mesh['x'=4,'y_hi'=2,'core'=2,'y_lo'=2,'z'=4] {'x','y_hi','y_lo','z'}, dimensions={0} | all-to-all | bytes 786432 | tf_op jit(solution)/shard_map/all_to_all | solution.py:219
  48.5 0.1 shard_map.77
  48.5 14.8 %all_to_all.17 = f32[64,3,4,128]{3,2,1,0:T(4,128)S(1)} all-to-all(f32[64,3,4,128]{3,2,1,0:T(4,128)S(1)} %bitcast.11), channel_id=1, replica_groups=mesh['x'=4,'y_hi'=2,'core'=2,'y_lo'=2,'z'=4] {'x','y_hi','y_lo','z'}, dimensions={0} | all-to-all | bytes 786432 | tf_op jit(solution)/shard_map/all_to_all | solution.py:219
  63.3 3.0 %collective-permute-start.1 = (f32[768,128]{1,0:T(8,128)S(1)}, f32[768,128]{1,0:T(8,128)S(1)}, u32[]{:S(2)}, u32[]{:S(2)}) collective-permute-start(f32[768,128]{1,0:T(8,128)S(1)} %bitcast.12), channel_id=1, source_target_pairs={{0,8},{8,0},{1,9},{9,1},{2,10},{10,2},{3,11},{11,3},{4,12},{12,4},... | collective-permute-start | bytes 1179656 | tf_op jit(solution)/shard_map/ppermute | solution.py:223
  66.3 1.3 %collective-permute-done.1.given_ref = f32[768,128]{1,0:T(8,128)S(1)} collective-permute-done((f32[768,128]{1,0:T(8,128)S(1)}, f32[768,128]{1,0:T(8,128)S(1)}, u32[]{:S(2)}, u32[]{:S(2)}) %collective-permute-start.1) | collective-permute-done | bytes 393248 | tf_op jit(solution)/shard_map/ppermute | solution.py:223
  67.7 1.0 %shard_map.78 = f32[440,440]{1,0:T(8,128)} custom-call(f32[768,128]{1,0:T(8,128)S(1)} %bitcast.13, f32[768,128]{1,0:T(8,128)S(1)} %collective-permute-done.1.given_ref), custom_call_target="tpu_custom_call" | custom-call | tf_op jit(solution)/shard_map/pallas_call | solution.py:295
Async XLA Ops:
  30.9 2.1 %collective-permute-start = (bf16[256,512]{1,0:T(8,128)(2,1)S(1)}, bf16[256,512]{1,0:T(8,128)(2,1)S(1)}, u32[]{:S(2)}, u32[]{:S(2)}) collective-permute-start(bf16[256,512]{1,0:T(8,128)(2,1)S(1)} %get-tuple-element.8.own_ref), channel_id=1, source_target_pairs={{0,8},{8,0},{1,9},{9,1},{2,10},{10,2},{3,11},{11,3},{4,12},{12,4},... | collective-permute-start | bytes 786440 | tf_op jit(solution)/shard_map/ppermute | solution.py:223
  63.3 4.4 %collective-permute-start.1 = (f32[768,128]{1,0:T(8,128)S(1)}, f32[768,128]{1,0:T(8,128)S(1)}, u32[]{:S(2)}, u32[]{:S(2)}) collective-permute-start(f32[768,128]{1,0:T(8,128)S(1)} %bitcast.12), channel_id=1, source_target_pairs={{0,8},{8,0},{1,9},{9,1},{2,10},{10,2},{3,11},{11,3},{4,12},{12,4},... | collective-permute-start | bytes 1179656 | tf_op jit(solution)/shard_map/ppermute | solution.py:223

commit v6 on v5

--- a/solution.py
+++ b/solution.py
@@ -167,18 +167,15 @@
         out_ref[d * 24 : (d + 1) * 24, :] = twice
 
 
-def place_kernel(kept_ref, given_ref, out_hbm, out_ref, sent):
+def density_rows(first, second, start, stop):
     lane = lane_index((8, LANES))
     upper = lax.broadcasted_iota(jnp.int32, (8, LANES), 0) < 4
-    copies = [
-        pltpu.make_async_copy(out_ref.at[n * 88 : (n + 1) * 88], out_hbm.at[n * 88 : (n + 1) * 88], sent.at[n]) for n in range(5)
-    ]
+    packed = FULL_TILES * 3
 
     def tiles(half, e):
         def got(t):
             return half[t * 8 : (t + 1) * 8, :]
 
-        packed = FULL_TILES * 3
         if e == FULL_TILES:
             rest = [got(packed + PACKED), got(packed + PACKED + 1)]
             return [rest[0], pltpu.roll(rest[0], 4, 0), rest[1], pltpu.roll(rest[1], 4, 0)]
@@ -193,26 +190,45 @@
                 strip = jnp.where((lane >= 8 * k) & (lane < 8 * k + 8), piece, strip)
         return [got(e * 3), got(e * 3 + 1), got(e * 3 + 2), strip]
 
-    def place(first, second):
-        below = None
-        for e in range(55):
-            if e < FULL_TILES:
-                row = tiles(first, e)
-            else:
-                above = tiles(first, e) if e == FULL_TILES else below
-                below = [pltpu.roll(x, 4, 0) for x in tiles(second, e - FULL_TILES)]
-                row = [jnp.where(upper, x, y) for x, y in zip(above, below)]
-            for chunk in range(3):
-                out_ref[e * 8 : (e + 1) * 8, chunk * LANES : (chunk + 1) * LANES] = row[chunk]
-            out_ref[e * 8 : (e + 1) * 8, 3 * LANES : 440] = row[3][:, 0:TAIL]
-            if e % 11 == 10:
-                copies[e // 11].start()
-
-    core = lax.axis_index("core")
-    pl.when(core == 0)(lambda: place(kept_ref, given_ref))
-    pl.when(core == 1)(lambda: place(given_ref, kept_ref))
+    def turned(e):
+        return [pltpu.roll(x, 4, 0) for x in tiles(second, e)]
+
+    below = None
+    for e in range(start, stop):
+        if e < FULL_TILES:
+            yield tiles(first, e)
+            continue
+        above = tiles(first, e) if e == FULL_TILES else turned(e - FULL_TILES - 1) if below is None else below
+        below = turned(e - FULL_TILES)
+        yield [jnp.where(upper, x, y) for x, y in zip(above, below)]
+
+
+def put_rows(first, second, start, stop, chunk, out_hbm, out_ref, sent):
+    copies = []
+    for n, row in enumerate(density_rows(first, second, start, stop)):
+        for c in range(3):
+            out_ref[n * 8 : (n + 1) * 8, c * LANES : (c + 1) * LANES] = row[c]
+        out_ref[n * 8 : (n + 1) * 8, 3 * LANES : 440] = row[3][:, 0:TAIL]
+        if n % chunk == chunk - 1:
+            here = slice((n - chunk + 1) * 8, (n + 1) * 8)
+            there = slice((start + n - chunk + 1) * 8, (start + n + 1) * 8)
+            copies.append(pltpu.make_async_copy(out_ref.at[here], out_hbm.at[there], sent.at[n // chunk]))
+            copies[-1].start()
     for copy in copies:
         copy.wait()
+
+
+def place_own_kernel(kept_ref, out_hbm, out_ref, sent):
+    core = lax.axis_index("core")
+    pl.when(core == 0)(lambda: put_rows(kept_ref, None, 0, FULL_TILES, 9, out_hbm, out_ref, sent))
+    pl.when(core == 1)(lambda: put_rows(None, kept_ref, FULL_TILES + 1, 55, 9, out_hbm, out_ref, sent))
+
+
+def place_other_kernel(kept_ref, given_ref, placed, out_hbm, out_ref, sent):
+    del placed
+    core = lax.axis_index("core")
+    pl.when(core == 0)(lambda: put_rows(kept_ref, given_ref, FULL_TILES, 55, 7, out_hbm, out_ref, sent))
+    pl.when(core == 1)(lambda: put_rows(given_ref, kept_ref, 0, FULL_TILES + 1, 7, out_hbm, out_ref, sent))
 
 
 def exchange(x, axes, shape):
@@ -292,14 +308,27 @@
     shares = exchange(share, ACROSS_CHIPS, (CHIPS, 3, 4, LANES))
     copies = call(sum_kernel, half, 1)(shares)
     slices = exchange(copies, ACROSS_CHIPS, (CHIPS, 3, 4, LANES))
+    hbm = pl.BlockSpec(memory_space=pltpu.HBM)
+    other_slices = to_other_core(slices)
+    density = jax.ShapeDtypeStruct((440, 440), f32)
+    placed = pl.pallas_call(
+        place_own_kernel,
+        out_shape=density,
+        in_specs=[vmem],
+        out_specs=hbm,
+        scratch_shapes=[pltpu.VMEM((FULL_TILES * 8, 440), f32), pltpu.SemaphoreType.DMA((3,))],
+        cost_estimate=pl.CostEstimate(flops=10**6, bytes_accessed=4 * 10**6, transcendentals=0),
+        compiler_params=PARAMS,
+    )(slices)
     return pl.pallas_call(
-        place_kernel,
-        out_shape=jax.ShapeDtypeStruct((440, 440), f32),
-        in_specs=[vmem] * 2,
-        out_specs=pl.BlockSpec(memory_space=pltpu.HBM),
-        scratch_shapes=[pltpu.VMEM((440, 440), f32), pltpu.SemaphoreType.DMA((5,))],
+        place_other_kernel,
+        out_shape=density,
+        in_specs=[vmem, vmem, hbm],
+        out_specs=hbm,
+        scratch_shapes=[pltpu.VMEM(((FULL_TILES + 1) * 8, 440), f32), pltpu.SemaphoreType.DMA((4,))],
+        input_output_aliases={2: 0},
         compiler_params=PARAMS,
-    )(slices, to_other_core(slices))
+    )(slices, other_slices, placed)
 
 
 def solution(mesh):

time: 68.9 us -> 68.7 us (level)
  waiting for transfers between devices: 1.35 us -> 0.53 us
    ppermute x2, waiting for transfers between devices: 1.35 us -> 0.53 us  [to_other_core(): return lax.ppermute(x, 'core', [(0, 1), (1, 0)])]
    pallas_call x1 -> x2, Pallas kernels: 0.98 us -> 1.64 us  [the longest x1 0.83 us: shards(): pl.pallas_call(place_other_kernel, out_shape=density, in_specs=[vmem, vme...]
  transfers between devices with their start and end apart: 2 -> 2, of which waited for: 1 -> 1; matrix products, arithmetic and copies ran while one was open for 0% -> 0% of each run, Pallas kernels for 2% -> 3%
where the time goes in v6:
time: 68.7 us; the launch traced here: 68.5 us
  blocking collectives  57.8 us (84%)
  Pallas kernels  5.64 us (8%)
  starting transfers between devices  3.85 us (6%)
  between operations  0.7 us (1%)
    all_to_all x3, blocking collectives, exchange(): lax.all_to_all(x.reshape(shape), axes, 0, 0, tiled=True).reshape(x.shape)  57.8 us
    ppermute x2, starting transfers between devices, to_other_core(): return lax.ppermute(x, 'core', [(0, 1), (1, 0)])  3.85 us
    pallas_call x1, Pallas kernels, shards(): pl.pallas_call(send_kernel, out_shape=jax.ShapeDtypeStruct((DEVICES * MES...  1.95 us
  transfers between devices with their start and end apart: 2, of which 1 were waited for; matrix products, arithmetic and copies ran while one was open for 0% of the time, Pallas kernels for 3%

profile of v6, /device:TPU:1, one launch (start us, length us, event | category | flops | bytes accessed | tf_op | source)
XLA Modules:
  0.0 68.5 jit_solution(1142515954458364386)
XLA Ops:
  0.7 2.0 %shard_map.73 = bf16[3072,128]{1,0:T(8,128)(2,1)S(1)} custom-call(s32[1,1]{1,0:T(1,128)S(6)} %copy.10.counts, bf16[1,4,440,128]{3,2,1,0:T(8,128)(2,1)} %bitcast.16, bf16[1,2,440,128]{3,2,1,0:T(8,128)(2,1)} %bitcast.17, s32[1,1,128]{2,1,0:T(1,128)} %pairs_final.1, s32[1,1,128]{2,1,0:T(1,128)} %pairs_initial.1, s32[1,4,440]{2,1,0:T(4,128)} %maps_final.1, ...), custom_call_target="tpu_custom_call" | custom-call | tf_op jit(solution)/shard_map/pallas_call | solution.py:259
  2.6 28.0 %all_to_all.15 = bf16[128,24,128]{2,1,0:T(8,128)(2,1)S(1)} all-to-all(bf16[128,24,128]{2,1,0:T(8,128)(2,1)S(1)} %bitcast.12), channel_id=1, replica_groups=mesh['x'=4,'y_hi'=2,'core'=2,'y_lo'=2,'z'=4] {'x','y_hi','core','y_lo','z'}, dimensions={0} | all-to-all | bytes 1572864 | tf_op jit(solution)/shard_map/all_to_all | solution.py:235
  30.7 0.2 shard_map.74
  30.9 0.8 %collective-permute-start = (bf16[256,512]{1,0:T(8,128)(2,1)S(1)}, bf16[256,512]{1,0:T(8,128)(2,1)S(1)}, u32[]{:S(2)}, u32[]{:S(2)}) collective-permute-start(bf16[256,512]{1,0:T(8,128)(2,1)S(1)} %get-tuple-element.8.own_ref), channel_id=1, source_target_pairs={{0,8},{8,0},{1,9},{9,1},{2,10},{10,2},{3,11},{11,3},{4,12},{12,4},... | collective-permute-start | bytes 786440 | tf_op jit(solution)/shard_map/ppermute | solution.py:239
  31.7 1.2 %shard_map.75.summed_ref = bf16[1024,256]{1,0:T(8,128)(2,1)S(1)} custom-call(f32[3072,128]{1,0:T(8,128)S(1)} %get-tuple-element.7.wide), custom_call_target="tpu_custom_call" | custom-call | flops 1000000000 | bytes 8000000 | tf_op jit(solution)/shard_map/pallas_call | solution.py:296
  32.9 0.0 collective-permute-done.other_ref
  32.9 0.5 shard_map.76
  33.5 15.0 %all_to_all.16 = f32[64,3,4,128]{3,2,1,0:T(4,128)S(1)} all-to-all(f32[64,3,4,128]{3,2,1,0:T(4,128)S(1)} %bitcast.15), channel_id=1, replica_groups=mesh['x'=4,'y_hi'=2,'core'=2,'y_lo'=2,'z'=4] {'x','y_hi','y_lo','z'}, dimensions={0} | all-to-all | bytes 786432 | tf_op jit(solution)/shard_map/all_to_all | solution.py:235
  48.5 0.1 shard_map.77
  48.5 14.8 %all_to_all.17 = f32[64,3,4,128]{3,2,1,0:T(4,128)S(1)} all-to-all(f32[64,3,4,128]{3,2,1,0:T(4,128)S(1)} %bitcast.14), channel_id=1, replica_groups=mesh['x'=4,'y_hi'=2,'core'=2,'y_lo'=2,'z'=4] {'x','y_hi','y_lo','z'}, dimensions={0} | all-to-all | bytes 786432 | tf_op jit(solution)/shard_map/all_to_all | solution.py:235
  63.3 3.0 %collective-permute-start.1 = (f32[768,128]{1,0:T(8,128)S(1)}, f32[768,128]{1,0:T(8,128)S(1)}, u32[]{:S(2)}, u32[]{:S(2)}) collective-permute-start(f32[768,128]{1,0:T(8,128)S(1)} %bitcast.8), channel_id=1, source_target_pairs={{0,8},{8,0},{1,9},{9,1},{2,10},{10,2},{3,11},{11,3},{4,12},{12,4},... | collective-permute-start | bytes 1179656 | tf_op jit(solution)/shard_map/ppermute | solution.py:239
  66.3 0.8 %shard_map.78.placed = f32[440,440]{1,0:T(8,128)} custom-call(f32[768,128]{1,0:T(8,128)S(1)} %bitcast.9), custom_call_target="tpu_custom_call" | custom-call | flops 1000000 | bytes 4000000 | tf_op jit(solution)/shard_map/pallas_call | solution.py:314
  67.2 0.5 collective-permute-done.1.given_ref
  67.7 0.8 %shard_map.79 = f32[440,440]{1,0:T(8,128)} custom-call(f32[768,128]{1,0:T(8,128)S(1)} %bitcast.10, f32[768,128]{1,0:T(8,128)S(1)} %collective-permute-done.1.given_ref, f32[440,440]{1,0:T(8,128)} %shard_map.78.placed), custom_call_target="tpu_custom_call", output_to_operand_aliasing={{}: (2, {})} | custom-call | tf_op jit(solution)/shard_map/pallas_call | solution.py:323
Async XLA Ops:
  30.9 2.1 %collective-permute-start = (bf16[256,512]{1,0:T(8,128)(2,1)S(1)}, bf16[256,512]{1,0:T(8,128)(2,1)S(1)}, u32[]{:S(2)}, u32[]{:S(2)}) collective-permute-start(bf16[256,512]{1,0:T(8,128)(2,1)S(1)} %get-tuple-element.8.own_ref), channel_id=1, source_target_pairs={{0,8},{8,0},{1,9},{9,1},{2,10},{10,2},{3,11},{11,3},{4,12},{12,4},... | collective-permute-start | bytes 786440 | tf_op jit(solution)/shard_map/ppermute | solution.py:239
  63.3 4.4 %collective-permute-start.1 = (f32[768,128]{1,0:T(8,128)S(1)}, f32[768,128]{1,0:T(8,128)S(1)}, u32[]{:S(2)}, u32[]{:S(2)}) collective-permute-start(f32[768,128]{1,0:T(8,128)S(1)} %bitcast.8), channel_id=1, source_target_pairs={{0,8},{8,0},{1,9},{9,1},{2,10},{10,2},{3,11},{11,3},{4,12},{12,4},... | collective-permute-start | bytes 1179656 | tf_op jit(solution)/shard_map/ppermute | solution.py:239

commit v7 on v6

--- a/solution.py
+++ b/solution.py
@@ -82,7 +82,7 @@
             initial[j * LANES : (j + 1) * LANES, chunk * LANES : (chunk + 1) * LANES] = part
 
 
-def times_kernel(wide, out_ref, pairs, final, met):
+def times_kernel(wide, own_ref, part_ref, out_ref, pairs, final, met):
     quarter = lane_index((LANES, LANES)) // 32
     for k in range(2):
         codes = jnp.zeros((LANES, LANES), jnp.float32)
@@ -121,17 +121,22 @@
     summed = jnp.dot(times, final[...], preferred_element_type=jnp.float32)
     high = summed.astype(jnp.bfloat16)
     low = (summed - high.astype(jnp.float32)).astype(jnp.bfloat16)
-    for other in range(2):
-        columns = slice(other * 256, (other + 1) * 256)
-        out_ref[other * 512 : other * 512 + 256, :] = high[:, columns]
-        out_ref[other * 512 + 256 : other * 512 + 512, :] = low[:, columns]
-
-
-def density_kernel(summed_ref, own_ref, other_ref, out_ref, full):
-    own, other = own_ref[...], other_ref[...]
-    full[...] = lax.dot_general(
+    own = own_ref[...]
+    part_ref[...] = lax.dot_general(
+        jnp.concatenate([high[:, 0:256], low[:, 0:256]], axis=0),
+        jnp.concatenate([own, own], axis=0),
+        (((0,), (0,)), ((), ())),
+        preferred_element_type=jnp.float32,
+    )
+    out_ref[0:256, :] = high[:, 256:512]
+    out_ref[256:512, :] = low[:, 256:512]
+
+
+def density_kernel(part_ref, summed_ref, other_ref, out_ref, full):
+    other = other_ref[...]
+    full[...] = part_ref[...] + lax.dot_general(
         summed_ref[...],
-        jnp.concatenate([own, own, other, other], axis=0),
+        jnp.concatenate([other, other], axis=0),
         (((0,), (0,)), ((), ())),
         preferred_element_type=jnp.float32,
     )
@@ -293,18 +298,18 @@
         1,
     )(received)
     other = to_other_core(own)
-    summed = call(
+    part, summed = call(
         times_kernel,
-        jax.ShapeDtypeStruct((1024, 256), bf16),
-        1,
+        [jax.ShapeDtypeStruct((256, 512), f32), jax.ShapeDtypeStruct((512, 256), bf16)],
+        2,
         [
             pltpu.VMEM((2 * LANES, LANES), f32),
             pltpu.VMEM((512, 512), bf16),
             pltpu.VMEM((4 * 256, LANES), f32),
         ],
         pl.CostEstimate(flops=10**9, bytes_accessed=8 * 10**6, transcendentals=0),
-    )(wide)
-    share = call(density_kernel, half, 3, [pltpu.VMEM((256, 512), f32)])(summed, own, other)
+    )(wide, own)
+    share = call(density_kernel, half, 3, [pltpu.VMEM((256, 512), f32)])(part, summed, other)
     shares = exchange(share, ACROSS_CHIPS, (CHIPS, 3, 4, LANES))
     copies = call(sum_kernel, half, 1)(shares)
     slices = exchange(copies, ACROSS_CHIPS, (CHIPS, 3, 4, LANES))

time: 68.7 us -> 68.9 us (level)
  no operation moved by 1% of the time
where the time goes in v7:
time: 68.9 us; the launch traced here: 68.7 us
  blocking collectives  58 us (84%)
  Pallas kernels  5.8 us (8%)
  starting transfers between devices  3.68 us (5%)
  between operations  0.69 us (1%)
    all_to_all x3, blocking collectives, exchange(): lax.all_to_all(x.reshape(shape), axes, 0, 0, tiled=True).reshape(x.shape)  58 us
    ppermute x2, starting transfers between devices, to_other_core(): return lax.ppermute(x, 'core', [(0, 1), (1, 0)])  3.68 us
    pallas_call x1, Pallas kernels, shards(): pl.pallas_call(send_kernel, out_shape=jax.ShapeDtypeStruct((DEVICES * MES...  1.95 us
    pallas_call x1, Pallas kernels, shards(): call(times_kernel, [jax.ShapeDtypeStruct((256, 512), f32), jax.ShapeDtype...  1.56 us
  transfers between devices with their start and end apart: 2, of which 1 were waited for; matrix products, arithmetic and copies ran while one was open for 0% of the time, Pallas kernels for 3%

profile of v7, /device:TPU:1, one launch (start us, length us, event | category | flops | bytes accessed | tf_op | source)
XLA Modules:
  0.0 68.7 jit_solution(17767203634135731504)
XLA Ops:
  0.7 2.0 %shard_map.73 = bf16[3072,128]{1,0:T(8,128)(2,1)S(1)} custom-call(s32[1,1]{1,0:T(1,128)S(6)} %copy.10.counts, bf16[1,4,440,128]{3,2,1,0:T(8,128)(2,1)} %bitcast.16, bf16[1,2,440,128]{3,2,1,0:T(8,128)(2,1)} %bitcast.17, s32[1,1,128]{2,1,0:T(1,128)} %pairs_final.1, s32[1,1,128]{2,1,0:T(1,128)} %pairs_initial.1, s32[1,4,440]{2,1,0:T(4,128)} %maps_final.1, ...), custom_call_target="tpu_custom_call" | custom-call | tf_op jit(solution)/shard_map/pallas_call | solution.py:264
  2.6 28.0 %all_to_all.15 = bf16[128,24,128]{2,1,0:T(8,128)(2,1)S(1)} all-to-all(bf16[128,24,128]{2,1,0:T(8,128)(2,1)S(1)} %bitcast.12), channel_id=1, replica_groups=mesh['x'=4,'y_hi'=2,'core'=2,'y_lo'=2,'z'=4] {'x','y_hi','core','y_lo','z'}, dimensions={0} | all-to-all | bytes 1572864 | tf_op jit(solution)/shard_map/all_to_all | solution.py:240
  30.7 0.2 shard_map.74
  30.9 0.8 %collective-permute-start = (bf16[256,512]{1,0:T(8,128)(2,1)S(1)}, bf16[256,512]{1,0:T(8,128)(2,1)S(1)}, u32[]{:S(2)}, u32[]{:S(2)}) collective-permute-start(bf16[256,512]{1,0:T(8,128)(2,1)S(1)} %get-tuple-element.10.own_ref), channel_id=1, source_target_pairs={{0,8},{8,0},{1,9},{9,1},{2,10},{10,2},{3,11},{11,3},{4,12},{12,4},... | collective-permute-start | bytes 786440 | tf_op jit(solution)/shard_map/ppermute | solution.py:244
  31.7 1.6 %shard_map.75 = (f32[256,512]{1,0:T(8,128)S(1)}, bf16[512,256]{1,0:T(8,128)(2,1)S(1)}) custom-call(f32[3072,128]{1,0:T(8,128)S(1)} %get-tuple-element.9.wide, bf16[256,512]{1,0:T(8,128)(2,1)S(1)} %get-tuple-element.10.own_ref), custom_call_target="tpu_custom_call" | custom-call | flops 1000000000 | bytes 8000000 | tf_op jit(solution)/shard_map/pallas_call | solution.py:301
  33.2 0.0 collective-permute-done.other_ref
  33.2 0.4 shard_map.76
  33.6 15.1 %all_to_all.16 = f32[64,3,4,128]{3,2,1,0:T(4,128)S(1)} all-to-all(f32[64,3,4,128]{3,2,1,0:T(4,128)S(1)} %bitcast.15), channel_id=1, replica_groups=mesh['x'=4,'y_hi'=2,'core'=2,'y_lo'=2,'z'=4] {'x','y_hi','y_lo','z'}, dimensions={0} | all-to-all | bytes 786432 | tf_op jit(solution)/shard_map/all_to_all | solution.py:240
  48.7 0.1 shard_map.77
  48.8 14.9 %all_to_all.17 = f32[64,3,4,128]{3,2,1,0:T(4,128)S(1)} all-to-all(f32[64,3,4,128]{3,2,1,0:T(4,128)S(1)} %bitcast.14), channel_id=1, replica_groups=mesh['x'=4,'y_hi'=2,'core'=2,'y_lo'=2,'z'=4] {'x','y_hi','y_lo','z'}, dimensions={0} | all-to-all | bytes 786432 | tf_op jit(solution)/shard_map/all_to_all | solution.py:240
  63.6 2.9 %collective-permute-start.1 = (f32[768,128]{1,0:T(8,128)S(1)}, f32[768,128]{1,0:T(8,128)S(1)}, u32[]{:S(2)}, u32[]{:S(2)}) collective-permute-start(f32[768,128]{1,0:T(8,128)S(1)} %bitcast.8), channel_id=1, source_target_pairs={{0,8},{8,0},{1,9},{9,1},{2,10},{10,2},{3,11},{11,3},{4,12},{12,4},... | collective-permute-start | bytes 1179656 | tf_op jit(solution)/shard_map/ppermute | solution.py:244
  66.5 0.8 %shard_map.78.placed = f32[440,440]{1,0:T(8,128)} custom-call(f32[768,128]{1,0:T(8,128)S(1)} %bitcast.9), custom_call_target="tpu_custom_call" | custom-call | flops 1000000 | bytes 4000000 | tf_op jit(solution)/shard_map/pallas_call | solution.py:319
  67.3 0.5 collective-permute-done.1.given_ref
  67.8 0.8 %shard_map.79 = f32[440,440]{1,0:T(8,128)} custom-call(f32[768,128]{1,0:T(8,128)S(1)} %bitcast.10, f32[768,128]{1,0:T(8,128)S(1)} %collective-permute-done.1.given_ref, f32[440,440]{1,0:T(8,128)} %shard_map.78.placed), custom_call_target="tpu_custom_call", output_to_operand_aliasing={{}: (2, {})} | custom-call | tf_op jit(solution)/shard_map/pallas_call | solution.py:328
Async XLA Ops:
  30.9 2.4 %collective-permute-start = (bf16[256,512]{1,0:T(8,128)(2,1)S(1)}, bf16[256,512]{1,0:T(8,128)(2,1)S(1)}, u32[]{:S(2)}, u32[]{:S(2)}) collective-permute-start(bf16[256,512]{1,0:T(8,128)(2,1)S(1)} %get-tuple-element.10.own_ref), channel_id=1, source_target_pairs={{0,8},{8,0},{1,9},{9,1},{2,10},{10,2},{3,11},{11,3},{4,12},{12,4},... | collective-permute-start | bytes 786440 | tf_op jit(solution)/shard_map/ppermute | solution.py:244
  63.6 4.2 %collective-permute-start.1 = (f32[768,128]{1,0:T(8,128)S(1)}, f32[768,128]{1,0:T(8,128)S(1)}, u32[]{:S(2)}, u32[]{:S(2)}) collective-permute-start(f32[768,128]{1,0:T(8,128)S(1)} %bitcast.8), channel_id=1, source_target_pairs={{0,8},{8,0},{1,9},{9,1},{2,10},{10,2},{3,11},{11,3},{4,12},{12,4},... | collective-permute-start | bytes 1179656 | tf_op jit(solution)/shard_map/ppermute | solution.py:244

commit v8 on v6

--- a/solution.py
+++ b/solution.py
@@ -54,9 +54,11 @@
     s_code = jnp.broadcast_to(s_code, (8, LANES))
     info = [pltpu.roll(code, (96 - 32 * m) % LANES, 1) for code in (q_code, s_code) for m in range(4)]
     last = lane_index((8, LANES)) >= 96
+    stored = lax.broadcasted_iota(jnp.int32, (440, 512), 0).astype(jnp.int16)
+    one, zero = jnp.ones((440, 512), jnp.bfloat16), jnp.zeros((440, 512), jnp.bfloat16)
     for j in range(6):
-        stored = lax.broadcasted_iota(jnp.int32, (440, 512), 0)
-        pick = jnp.where(stored == maps[j : j + 1, :], 1.0, 0.0).astype(jnp.bfloat16)
+        wanted = jnp.broadcast_to(maps[j : j + 1, :], (440, 512)).astype(jnp.int16)
+        pick = jnp.where(stored == wanted, one, zero)
         ordered = lax.dot_general(blocks[j], pick, (((0,), (0,)), ((), ())), preferred_element_type=jnp.float32)
         for chunk in range(4):
             part = ordered[:, chunk * LANES : (chunk + 1) * LANES]
@@ -74,15 +76,19 @@
     out_ref[...] = wide[...].astype(jnp.bfloat16)
 
 
-def widen_kernel(in_ref, wide, initial):
-    wide[...] = in_ref[...].astype(jnp.float32)
+def initial_kernel(in_ref, initial, wide):
+    for d in range(0, DEVICES, 2):
+        both = in_ref[d * MESSAGE : (d + 2) * MESSAGE, :].astype(jnp.float32)
+        wide[d * 8 : (d + 1) * 8, :] = both[FINAL_ROWS:MESSAGE]
+        wide[(d + 1) * 8 : (d + 2) * 8, :] = both[MESSAGE + FINAL_ROWS :]
     for j in range(2):
         for chunk in range(4):
-            part = wide[pl.ds(FINAL_ROWS + j * 4 + chunk, DEVICES, stride=MESSAGE), :].astype(jnp.bfloat16)
+            part = wide[pl.ds(j * 4 + chunk, DEVICES, stride=8), :].astype(jnp.bfloat16)
             initial[j * LANES : (j + 1) * LANES, chunk * LANES : (chunk + 1) * LANES] = part
 
 
-def times_kernel(wide, out_ref, pairs, final, met):
+def times_kernel(in_ref, out_ref, wide, pairs, final, met):
+    wide[...] = in_ref[...].astype(jnp.float32)
     quarter = lane_index((LANES, LANES)) // 32
     for k in range(2):
         codes = jnp.zeros((LANES, LANES), jnp.float32)
@@ -287,10 +293,8 @@
         )
     )
     received = exchange(messages, ALL, (DEVICES, MESSAGE, LANES))
-    wide, own = call(
-        widen_kernel,
-        [jax.ShapeDtypeStruct((DEVICES * MESSAGE, LANES), f32), jax.ShapeDtypeStruct((256, 512), bf16)],
-        1,
+    own = call(
+        initial_kernel, jax.ShapeDtypeStruct((256, 512), bf16), 1, [pltpu.VMEM((DEVICES * 8, LANES), f32)]
     )(received)
     other = to_other_core(own)
     summed = call(
@@ -298,12 +302,13 @@
         jax.ShapeDtypeStruct((1024, 256), bf16),
         1,
         [
+            pltpu.VMEM((DEVICES * MESSAGE, LANES), f32),
             pltpu.VMEM((2 * LANES, LANES), f32),
             pltpu.VMEM((512, 512), bf16),
             pltpu.VMEM((4 * 256, LANES), f32),
         ],
         pl.CostEstimate(flops=10**9, bytes_accessed=8 * 10**6, transcendentals=0),
-    )(wide)
+    )(received)
     share = call(density_kernel, half, 3, [pltpu.VMEM((256, 512), f32)])(summed, own, other)
     shares = exchange(share, ACROSS_CHIPS, (CHIPS, 3, 4, LANES))
     copies = call(sum_kernel, half, 1)(shares)

time: 68.7 us -> 68.6 us (level)
  no operation moved by 1% of the time
where the time goes in v8:
time: 68.6 us; the launch traced here: 68.4 us
  blocking collectives  57.9 us (84%)
  Pallas kernels  5.52 us (8%)
  starting transfers between devices  3.75 us (5%)
  between operations  0.7 us (1%)
    all_to_all x3, blocking collectives, exchange(): lax.all_to_all(x.reshape(shape), axes, 0, 0, tiled=True).reshape(x.shape)  57.9 us
    ppermute x2, starting transfers between devices, to_other_core(): return lax.ppermute(x, 'core', [(0, 1), (1, 0)])  3.75 us
    pallas_call x1, Pallas kernels, shards(): pl.pallas_call(send_kernel, out_shape=jax.ShapeDtypeStruct((DEVICES * MES...  1.87 us
  transfers between devices with their start and end apart: 2, of which 1 were waited for; matrix products, arithmetic and copies ran while one was open for 0% of the time, Pallas kernels for 3%

profile of v8, /device:TPU:1, one launch (start us, length us, event | category | flops | bytes accessed | tf_op | source)
XLA Modules:
  0.0 68.4 jit_solution(6917205682215656119)
XLA Ops:
  0.7 1.9 %shard_map.73 = bf16[3072,128]{1,0:T(8,128)(2,1)S(1)} custom-call(s32[1,1]{1,0:T(1,128)S(6)} %copy.10.counts, bf16[1,4,440,128]{3,2,1,0:T(8,128)(2,1)} %bitcast.17, bf16[1,2,440,128]{3,2,1,0:T(8,128)(2,1)} %bitcast.18, s32[1,1,128]{2,1,0:T(1,128)} %pairs_final.1, s32[1,1,128]{2,1,0:T(1,128)} %pairs_initial.1, s32[1,4,440]{2,1,0:T(4,128)} %maps_final.1, ...), custom_call_target="tpu_custom_call" | custom-call | tf_op jit(solution)/shard_map/pallas_call | solution.py:265
  2.5 28.0 %all_to_all.15 = bf16[128,24,128]{2,1,0:T(8,128)(2,1)S(1)} all-to-all(bf16[128,24,128]{2,1,0:T(8,128)(2,1)S(1)} %bitcast.13), channel_id=1, replica_groups=mesh['x'=4,'y_hi'=2,'core'=2,'y_lo'=2,'z'=4] {'x','y_hi','core','y_lo','z'}, dimensions={0} | all-to-all | bytes 1572864 | tf_op jit(solution)/shard_map/all_to_all | solution.py:241
  30.6 0.1 shard_map.75.own_ref
  30.7 0.8 %collective-permute-start = (bf16[256,512]{1,0:T(8,128)(2,1)S(1)}, bf16[256,512]{1,0:T(8,128)(2,1)S(1)}, u32[]{:S(2)}, u32[]{:S(2)}) collective-permute-start(bf16[256,512]{1,0:T(8,128)(2,1)S(1)} %shard_map.75.own_ref), channel_id=1, source_target_pairs={{0,8},{8,0},{1,9},{9,1},{2,10},{10,2},{3,11},{11,3},{4,12},{12,4},... | collective-permute-start | bytes 786440 | tf_op jit(solution)/shard_map/ppermute | solution.py:245
  31.5 1.3 %shard_map.74.summed_ref = bf16[1024,256]{1,0:T(8,128)(2,1)S(1)} custom-call(bf16[3072,128]{1,0:T(8,128)(2,1)S(1)} %bitcast.12), custom_call_target="tpu_custom_call" | custom-call | flops 1000000000 | bytes 8000000 | tf_op jit(solution)/shard_map/pallas_call | solution.py:300
  32.8 0.0 collective-permute-done.other_ref
  32.8 0.5 shard_map.76
  33.4 15.0 %all_to_all.16 = f32[64,3,4,128]{3,2,1,0:T(4,128)S(1)} all-to-all(f32[64,3,4,128]{3,2,1,0:T(4,128)S(1)} %bitcast.16), channel_id=1, replica_groups=mesh['x'=4,'y_hi'=2,'core'=2,'y_lo'=2,'z'=4] {'x','y_hi','y_lo','z'}, dimensions={0} | all-to-all | bytes 786432 | tf_op jit(solution)/shard_map/all_to_all | solution.py:241
  48.4 0.1 shard_map.77
  48.5 14.8 %all_to_all.17 = f32[64,3,4,128]{3,2,1,0:T(4,128)S(1)} all-to-all(f32[64,3,4,128]{3,2,1,0:T(4,128)S(1)} %bitcast.15), channel_id=1, replica_groups=mesh['x'=4,'y_hi'=2,'core'=2,'y_lo'=2,'z'=4] {'x','y_hi','y_lo','z'}, dimensions={0} | all-to-all | bytes 786432 | tf_op jit(solution)/shard_map/all_to_all | solution.py:241
  63.3 2.9 %collective-permute-start.1 = (f32[768,128]{1,0:T(8,128)S(1)}, f32[768,128]{1,0:T(8,128)S(1)}, u32[]{:S(2)}, u32[]{:S(2)}) collective-permute-start(f32[768,128]{1,0:T(8,128)S(1)} %bitcast.8), channel_id=1, source_target_pairs={{0,8},{8,0},{1,9},{9,1},{2,10},{10,2},{3,11},{11,3},{4,12},{12,4},... | collective-permute-start | bytes 1179656 | tf_op jit(solution)/shard_map/ppermute | solution.py:245
  66.2 0.8 %shard_map.78.placed = f32[440,440]{1,0:T(8,128)} custom-call(f32[768,128]{1,0:T(8,128)S(1)} %bitcast.9), custom_call_target="tpu_custom_call" | custom-call | flops 1000000 | bytes 4000000 | tf_op jit(solution)/shard_map/pallas_call | solution.py:319
  67.0 0.5 collective-permute-done.1.given_ref
  67.6 0.8 %shard_map.79 = f32[440,440]{1,0:T(8,128)} custom-call(f32[768,128]{1,0:T(8,128)S(1)} %bitcast.10, f32[768,128]{1,0:T(8,128)S(1)} %collective-permute-done.1.given_ref, f32[440,440]{1,0:T(8,128)} %shard_map.78.placed), custom_call_target="tpu_custom_call", output_to_operand_aliasing={{}: (2, {})} | custom-call | tf_op jit(solution)/shard_map/pallas_call | solution.py:328
Async XLA Ops:
  30.7 2.1 %collective-permute-start = (bf16[256,512]{1,0:T(8,128)(2,1)S(1)}, bf16[256,512]{1,0:T(8,128)(2,1)S(1)}, u32[]{:S(2)}, u32[]{:S(2)}) collective-permute-start(bf16[256,512]{1,0:T(8,128)(2,1)S(1)} %shard_map.75.own_ref), channel_id=1, source_target_pairs={{0,8},{8,0},{1,9},{9,1},{2,10},{10,2},{3,11},{11,3},{4,12},{12,4},... | collective-permute-start | bytes 786440 | tf_op jit(solution)/shard_map/ppermute | solution.py:245
  63.3 4.3 %collective-permute-start.1 = (f32[768,128]{1,0:T(8,128)S(1)}, f32[768,128]{1,0:T(8,128)S(1)}, u32[]{:S(2)}, u32[]{:S(2)}) collective-permute-start(f32[768,128]{1,0:T(8,128)S(1)} %bitcast.8), channel_id=1, source_target_pairs={{0,8},{8,0},{1,9},{9,1},{2,10},{10,2},{3,11},{11,3},{4,12},{12,4},... | collective-permute-start | bytes 1179656 | tf_op jit(solution)/shard_map/ppermute | solution.py:245

commit v9 on v8

--- a/solution.py
+++ b/solution.py
@@ -224,17 +224,10 @@
         copy.wait()
 
 
-def place_own_kernel(kept_ref, out_hbm, out_ref, sent):
+def place_kernel(kept_ref, given_ref, out_hbm, out_ref, sent):
     core = lax.axis_index("core")
-    pl.when(core == 0)(lambda: put_rows(kept_ref, None, 0, FULL_TILES, 9, out_hbm, out_ref, sent))
-    pl.when(core == 1)(lambda: put_rows(None, kept_ref, FULL_TILES + 1, 55, 9, out_hbm, out_ref, sent))
-
-
-def place_other_kernel(kept_ref, given_ref, placed, out_hbm, out_ref, sent):
-    del placed
-    core = lax.axis_index("core")
-    pl.when(core == 0)(lambda: put_rows(kept_ref, given_ref, FULL_TILES, 55, 7, out_hbm, out_ref, sent))
-    pl.when(core == 1)(lambda: put_rows(given_ref, kept_ref, 0, FULL_TILES + 1, 7, out_hbm, out_ref, sent))
+    pl.when(core == 0)(lambda: put_rows(kept_ref, given_ref, 0, 55, 11, out_hbm, out_ref, sent))
+    pl.when(core == 1)(lambda: put_rows(given_ref, kept_ref, 0, 55, 11, out_hbm, out_ref, sent))
 
 
 def exchange(x, axes, shape):
@@ -314,26 +307,14 @@
     copies = call(sum_kernel, half, 1)(shares)
     slices = exchange(copies, ACROSS_CHIPS, (CHIPS, 3, 4, LANES))
     hbm = pl.BlockSpec(memory_space=pltpu.HBM)
-    other_slices = to_other_core(slices)
-    density = jax.ShapeDtypeStruct((440, 440), f32)
-    placed = pl.pallas_call(
-        place_own_kernel,
-        out_shape=density,
-        in_specs=[vmem],
+    return pl.pallas_call(
+        place_kernel,
+        out_shape=jax.ShapeDtypeStruct((440, 440), f32),
+        in_specs=[vmem, vmem],
         out_specs=hbm,
-        scratch_shapes=[pltpu.VMEM((FULL_TILES * 8, 440), f32), pltpu.SemaphoreType.DMA((3,))],
-        cost_estimate=pl.CostEstimate(flops=10**6, bytes_accessed=4 * 10**6, transcendentals=0),
+        scratch_shapes=[pltpu.VMEM((440, 440), f32), pltpu.SemaphoreType.DMA((5,))],
         compiler_params=PARAMS,
-    )(slices)
-    return pl.pallas_call(
-        place_other_kernel,
-        out_shape=density,
-        in_specs=[vmem, vmem, hbm],
-        out_specs=hbm,
-        scratch_shapes=[pltpu.VMEM(((FULL_TILES + 1) * 8, 440), f32), pltpu.SemaphoreType.DMA((4,))],
-        input_output_aliases={2: 0},
-        compiler_params=PARAMS,
-    )(slices, other_slices, placed)
+    )(slices, to_other_core(slices))
 
 
 def solution(mesh):

time: 68.6 us -> 68.8 us (level)
  waiting for transfers between devices: 0.53 us -> 1.35 us
    ppermute x2, waiting for transfers between devices: 0.53 us -> 1.35 us  [to_other_core(): return lax.ppermute(x, 'core', [(0, 1), (1, 0)])]
    pallas_call x2 -> x1, Pallas kernels: 1.64 us -> 0.98 us  [shards(): pl.pallas_call(place_kernel, out_shape=jax.ShapeDtypeStruct((440, 440), f...]
  transfers between devices with their start and end apart: 2 -> 2, of which waited for: 1 -> 1; matrix products, arithmetic and copies ran while one was open for 0% -> 0% of each run, Pallas kernels for 3% -> 2%
where the time goes in v9:
time: 68.8 us; the launch traced here: 68.5 us
  blocking collectives  57.9 us (84%)
  Pallas kernels  4.86 us (7%)
  starting transfers between devices  3.75 us (5%)
  waiting for transfers between devices  1.35 us (2%)
  between operations  0.69 us (1%)
    all_to_all x3, blocking collectives, exchange(): lax.all_to_all(x.reshape(shape), axes, 0, 0, tiled=True).reshape(x.shape)  57.9 us
    ppermute x2, starting transfers between devices, to_other_core(): return lax.ppermute(x, 'core', [(0, 1), (1, 0)])  3.75 us
    pallas_call x1, Pallas kernels, shards(): pl.pallas_call(send_kernel, out_shape=jax.ShapeDtypeStruct((DEVICES * MES...  1.87 us
  transfers between devices with their start and end apart: 2, of which 1 were waited for; matrix products, arithmetic and copies ran while one was open for 0% of the time, Pallas kernels for 2%

profile of v9, /device:TPU:1, one launch (start us, length us, event | category | flops | bytes accessed | tf_op | source)
XLA Modules:
  0.0 68.5 jit_solution(9531593571503109367)
XLA Ops:
  0.7 1.9 %shard_map.73 = bf16[3072,128]{1,0:T(8,128)(2,1)S(1)} custom-call(s32[1,1]{1,0:T(1,128)S(6)} %copy.8.counts, bf16[1,4,440,128]{3,2,1,0:T(8,128)(2,1)} %bitcast.16, bf16[1,2,440,128]{3,2,1,0:T(8,128)(2,1)} %bitcast.17, s32[1,1,128]{2,1,0:T(1,128)} %pairs_final.1, s32[1,1,128]{2,1,0:T(1,128)} %pairs_initial.1, s32[1,4,440]{2,1,0:T(4,128)} %maps_final.1, ...), custom_call_target="tpu_custom_call" | custom-call | tf_op jit(solution)/shard_map/pallas_call | solution.py:258
  2.5 28.0 %all_to_all.15 = bf16[128,24,128]{2,1,0:T(8,128)(2,1)S(1)} all-to-all(bf16[128,24,128]{2,1,0:T(8,128)(2,1)S(1)} %bitcast.10), channel_id=1, replica_groups=mesh['x'=4,'y_hi'=2,'core'=2,'y_lo'=2,'z'=4] {'x','y_hi','core','y_lo','z'}, dimensions={0} | all-to-all | bytes 1572864 | tf_op jit(solution)/shard_map/all_to_all | solution.py:234
  30.6 0.1 shard_map.75.own_ref
  30.7 0.8 %collective-permute-start = (bf16[256,512]{1,0:T(8,128)(2,1)S(1)}, bf16[256,512]{1,0:T(8,128)(2,1)S(1)}, u32[]{:S(2)}, u32[]{:S(2)}) collective-permute-start(bf16[256,512]{1,0:T(8,128)(2,1)S(1)} %shard_map.75.own_ref), channel_id=1, source_target_pairs={{0,8},{8,0},{1,9},{9,1},{2,10},{10,2},{3,11},{11,3},{4,12},{12,4},... | collective-permute-start | bytes 786440 | tf_op jit(solution)/shard_map/ppermute | solution.py:238
  31.5 1.3 %shard_map.74.summed_ref = bf16[1024,256]{1,0:T(8,128)(2,1)S(1)} custom-call(bf16[3072,128]{1,0:T(8,128)(2,1)S(1)} %bitcast.9), custom_call_target="tpu_custom_call" | custom-call | flops 1000000000 | bytes 8000000 | tf_op jit(solution)/shard_map/pallas_call | solution.py:293
  32.8 0.0 collective-permute-done.other_ref
  32.8 0.5 shard_map.76
  33.4 15.0 %all_to_all.16 = f32[64,3,4,128]{3,2,1,0:T(4,128)S(1)} all-to-all(f32[64,3,4,128]{3,2,1,0:T(4,128)S(1)} %bitcast.15), channel_id=1, replica_groups=mesh['x'=4,'y_hi'=2,'core'=2,'y_lo'=2,'z'=4] {'x','y_hi','y_lo','z'}, dimensions={0} | all-to-all | bytes 786432 | tf_op jit(solution)/shard_map/all_to_all | solution.py:234
  48.4 0.1 shard_map.77
  48.5 14.8 %all_to_all.17 = f32[64,3,4,128]{3,2,1,0:T(4,128)S(1)} all-to-all(f32[64,3,4,128]{3,2,1,0:T(4,128)S(1)} %bitcast.12), channel_id=1, replica_groups=mesh['x'=4,'y_hi'=2,'core'=2,'y_lo'=2,'z'=4] {'x','y_hi','y_lo','z'}, dimensions={0} | all-to-all | bytes 786432 | tf_op jit(solution)/shard_map/all_to_all | solution.py:234
  63.3 2.9 %collective-permute-start.1 = (f32[768,128]{1,0:T(8,128)S(1)}, f32[768,128]{1,0:T(8,128)S(1)}, u32[]{:S(2)}, u32[]{:S(2)}) collective-permute-start(f32[768,128]{1,0:T(8,128)S(1)} %bitcast.13), channel_id=1, source_target_pairs={{0,8},{8,0},{1,9},{9,1},{2,10},{10,2},{3,11},{11,3},{4,12},{12,4},... | collective-permute-start | bytes 1179656 | tf_op jit(solution)/shard_map/ppermute | solution.py:238
  66.2 1.3 %collective-permute-done.1.given_ref = f32[768,128]{1,0:T(8,128)S(1)} collective-permute-done((f32[768,128]{1,0:T(8,128)S(1)}, f32[768,128]{1,0:T(8,128)S(1)}, u32[]{:S(2)}, u32[]{:S(2)}) %collective-permute-start.1) | collective-permute-done | bytes 393248 | tf_op jit(solution)/shard_map/ppermute | solution.py:238
  67.6 1.0 %shard_map.78 = f32[440,440]{1,0:T(8,128)} custom-call(f32[768,128]{1,0:T(8,128)S(1)} %bitcast.14, f32[768,128]{1,0:T(8,128)S(1)} %collective-permute-done.1.given_ref), custom_call_target="tpu_custom_call" | custom-call | tf_op jit(solution)/shard_map/pallas_call | solution.py:310
Async XLA Ops:
  30.7 2.1 %collective-permute-start = (bf16[256,512]{1,0:T(8,128)(2,1)S(1)}, bf16[256,512]{1,0:T(8,128)(2,1)S(1)}, u32[]{:S(2)}, u32[]{:S(2)}) collective-permute-start(bf16[256,512]{1,0:T(8,128)(2,1)S(1)} %shard_map.75.own_ref), channel_id=1, source_target_pairs={{0,8},{8,0},{1,9},{9,1},{2,10},{10,2},{3,11},{11,3},{4,12},{12,4},... | collective-permute-start | bytes 786440 | tf_op jit(solution)/shard_map/ppermute | solution.py:238
  63.3 4.3 %collective-permute-start.1 = (f32[768,128]{1,0:T(8,128)S(1)}, f32[768,128]{1,0:T(8,128)S(1)}, u32[]{:S(2)}, u32[]{:S(2)}) collective-permute-start(f32[768,128]{1,0:T(8,128)S(1)} %bitcast.13), channel_id=1, source_target_pairs={{0,8},{8,0},{1,9},{9,1},{2,10},{10,2},{3,11},{11,3},{4,12},{12,4},... | collective-permute-start | bytes 1179656 | tf_op jit(solution)/shard_map/ppermute | solution.py:238

commit v10 on v7

--- a/solution.py
+++ b/solution.py
@@ -54,9 +54,11 @@
     s_code = jnp.broadcast_to(s_code, (8, LANES))
     info = [pltpu.roll(code, (96 - 32 * m) % LANES, 1) for code in (q_code, s_code) for m in range(4)]
     last = lane_index((8, LANES)) >= 96
+    stored = lax.broadcasted_iota(jnp.int32, (440, 512), 0).astype(jnp.int16)
+    one, zero = jnp.ones((440, 512), jnp.bfloat16), jnp.zeros((440, 512), jnp.bfloat16)
     for j in range(6):
-        stored = lax.broadcasted_iota(jnp.int32, (440, 512), 0)
-        pick = jnp.where(stored == maps[j : j + 1, :], 1.0, 0.0).astype(jnp.bfloat16)
+        wanted = jnp.broadcast_to(maps[j : j + 1, :], (440, 512)).astype(jnp.int16)
+        pick = jnp.where(stored == wanted, one, zero)
         ordered = lax.dot_general(blocks[j], pick, (((0,), (0,)), ((), ())), preferred_element_type=jnp.float32)
         for chunk in range(4):
             part = ordered[:, chunk * LANES : (chunk + 1) * LANES]
@@ -74,15 +76,19 @@
     out_ref[...] = wide[...].astype(jnp.bfloat16)
 
 
-def widen_kernel(in_ref, wide, initial):
-    wide[...] = in_ref[...].astype(jnp.float32)
+def initial_kernel(in_ref, initial, wide):
+    for d in range(0, DEVICES, 2):
+        both = in_ref[d * MESSAGE : (d + 2) * MESSAGE, :].astype(jnp.float32)
+        wide[d * 8 : (d + 1) * 8, :] = both[FINAL_ROWS:MESSAGE]
+        wide[(d + 1) * 8 : (d + 2) * 8, :] = both[MESSAGE + FINAL_ROWS :]
     for j in range(2):
         for chunk in range(4):
-            part = wide[pl.ds(FINAL_ROWS + j * 4 + chunk, DEVICES, stride=MESSAGE), :].astype(jnp.bfloat16)
+            part = wide[pl.ds(j * 4 + chunk, DEVICES, stride=8), :].astype(jnp.bfloat16)
             initial[j * LANES : (j + 1) * LANES, chunk * LANES : (chunk + 1) * LANES] = part
 
 
-def times_kernel(wide, own_ref, part_ref, out_ref, pairs, final, met):
+def times_kernel(in_ref, own_ref, part_ref, out_ref, wide, pairs, final, met):
+    wide[...] = in_ref[...].astype(jnp.float32)
     quarter = lane_index((LANES, LANES)) // 32
     for k in range(2):
         codes = jnp.zeros((LANES, LANES), jnp.float32)
@@ -101,18 +107,17 @@
     def one_hot(slots):
         return jnp.where(code == slots, 1.0, 0.0).astype(jnp.bfloat16)
 
-    for c in range(8):
-        for g in range(4):
+    zero = jnp.zeros((32, LANES), jnp.bfloat16)
+    for g in range(4):
+        for c in range(8):
             cells = []
-            for d in range(g * 32 + c, g * 32 + 32, 8):
-                cells.append(
-                    lax.dot_general(
-                        one_hot(pairs[LANES + d : LANES + d + 1, :]),
-                        one_hot(pairs[d : d + 1, :]),
-                        (((1,), (1,)), ((), ())),
-                        preferred_element_type=jnp.float32,
-                    )
+            for d in range(g * 32 + c, g * 32 + 32, 16):
+                left = jnp.concatenate([one_hot(pairs[LANES + e : LANES + e + 1, :]) for e in (d, d + 8)], axis=1)
+                q = [one_hot(pairs[e : e + 1, :]) for e in (d, d + 8)]
+                right = jnp.concatenate(
+                    [jnp.concatenate([q[0], zero], axis=1), jnp.concatenate([zero, q[1]], axis=1)], axis=0
                 )
+                cells.append(lax.dot_general(left, right, (((1,), (1,)), ((), ())), preferred_element_type=jnp.float32))
             cells = jnp.concatenate(cells, axis=1)
             for j in range(2):
                 met[pl.ds(g * 256 + j * LANES + c, 16, stride=8), :] = cells[j * 16 : (j + 1) * 16]
@@ -292,10 +297,8 @@
         )
     )
     received = exchange(messages, ALL, (DEVICES, MESSAGE, LANES))
-    wide, own = call(
-        widen_kernel,
-        [jax.ShapeDtypeStruct((DEVICES * MESSAGE, LANES), f32), jax.ShapeDtypeStruct((256, 512), bf16)],
-        1,
+    own = call(
+        initial_kernel, jax.ShapeDtypeStruct((256, 512), bf16), 1, [pltpu.VMEM((DEVICES * 8, LANES), f32)]
     )(received)
     other = to_other_core(own)
     part, summed = call(
@@ -303,12 +306,13 @@
         [jax.ShapeDtypeStruct((256, 512), f32), jax.ShapeDtypeStruct((512, 256), bf16)],
         2,
         [
+            pltpu.VMEM((DEVICES * MESSAGE, LANES), f32),
             pltpu.VMEM((2 * LANES, LANES), f32),
             pltpu.VMEM((512, 512), bf16),
             pltpu.VMEM((4 * 256, LANES), f32),
         ],
         pl.CostEstimate(flops=10**9, bytes_accessed=8 * 10**6, transcendentals=0),
-    )(wide, own)
+    )(received, own)
     share = call(density_kernel, half, 3, [pltpu.VMEM((256, 512), f32)])(part, summed, other)
     shares = exchange(share, ACROSS_CHIPS, (CHIPS, 3, 4, LANES))
     copies = call(sum_kernel, half, 1)(shares)

time: 68.9 us -> 68.6 us (level)
  no operation moved by 1% of the time
where the time goes in v10:
time: 68.6 us; the launch traced here: 68.4 us
  blocking collectives  58 us (85%)
  Pallas kernels  5.56 us (8%)
  starting transfers between devices  3.68 us (5%)
  between operations  0.69 us (1%)
    all_to_all x3, blocking collectives, exchange(): lax.all_to_all(x.reshape(shape), axes, 0, 0, tiled=True).reshape(x.shape)  58 us
    ppermute x2, starting transfers between devices, to_other_core(): return lax.ppermute(x, 'core', [(0, 1), (1, 0)])  3.68 us
    pallas_call x1, Pallas kernels, shards(): pl.pallas_call(send_kernel, out_shape=jax.ShapeDtypeStruct((DEVICES * MES...  1.87 us
    pallas_call x1, Pallas kernels, shards(): call(times_kernel, [jax.ShapeDtypeStruct((256, 512), f32), jax.ShapeDtype...  1.46 us
  transfers between devices with their start and end apart: 2, of which 1 were waited for; matrix products, arithmetic and copies ran while one was open for 0% of the time, Pallas kernels for 3%

profile of v10, /device:TPU:1, one launch (start us, length us, event | category | flops | bytes accessed | tf_op | source)
XLA Modules:
  0.0 68.4 jit_solution(9750351302925840244)
XLA Ops:
  0.7 1.9 %shard_map.73 = bf16[3072,128]{1,0:T(8,128)(2,1)S(1)} custom-call(s32[1,1]{1,0:T(1,128)S(6)} %copy.10.counts, bf16[1,4,440,128]{3,2,1,0:T(8,128)(2,1)} %bitcast.17, bf16[1,2,440,128]{3,2,1,0:T(8,128)(2,1)} %bitcast.18, s32[1,1,128]{2,1,0:T(1,128)} %pairs_final.1, s32[1,1,128]{2,1,0:T(1,128)} %pairs_initial.1, s32[1,4,440]{2,1,0:T(4,128)} %maps_final.1, ...), custom_call_target="tpu_custom_call" | custom-call | tf_op jit(solution)/shard_map/pallas_call | solution.py:269
  2.5 28.0 %all_to_all.15 = bf16[128,24,128]{2,1,0:T(8,128)(2,1)S(1)} all-to-all(bf16[128,24,128]{2,1,0:T(8,128)(2,1)S(1)} %bitcast.13), channel_id=1, replica_groups=mesh['x'=4,'y_hi'=2,'core'=2,'y_lo'=2,'z'=4] {'x','y_hi','core','y_lo','z'}, dimensions={0} | all-to-all | bytes 1572864 | tf_op jit(solution)/shard_map/all_to_all | solution.py:245
  30.6 0.1 shard_map.74.own_ref
  30.7 0.8 %collective-permute-start = (bf16[256,512]{1,0:T(8,128)(2,1)S(1)}, bf16[256,512]{1,0:T(8,128)(2,1)S(1)}, u32[]{:S(2)}, u32[]{:S(2)}) collective-permute-start(bf16[256,512]{1,0:T(8,128)(2,1)S(1)} %shard_map.74.own_ref), channel_id=1, source_target_pairs={{0,8},{8,0},{1,9},{9,1},{2,10},{10,2},{3,11},{11,3},{4,12},{12,4},... | collective-permute-start | bytes 786440 | tf_op jit(solution)/shard_map/ppermute | solution.py:249
  31.5 1.5 %shard_map.75 = (f32[256,512]{1,0:T(8,128)S(1)}, bf16[512,256]{1,0:T(8,128)(2,1)S(1)}) custom-call(bf16[3072,128]{1,0:T(8,128)(2,1)S(1)} %bitcast.12, bf16[256,512]{1,0:T(8,128)(2,1)S(1)} %shard_map.74.own_ref), custom_call_target="tpu_custom_call" | custom-call | flops 1000000000 | bytes 8000000 | tf_op jit(solution)/shard_map/pallas_call | solution.py:304
  33.0 0.0 collective-permute-done.other_ref
  33.0 0.4 shard_map.76
  33.4 15.1 %all_to_all.16 = f32[64,3,4,128]{3,2,1,0:T(4,128)S(1)} all-to-all(f32[64,3,4,128]{3,2,1,0:T(4,128)S(1)} %bitcast.16), channel_id=1, replica_groups=mesh['x'=4,'y_hi'=2,'core'=2,'y_lo'=2,'z'=4] {'x','y_hi','y_lo','z'}, dimensions={0} | all-to-all | bytes 786432 | tf_op jit(solution)/shard_map/all_to_all | solution.py:245
  48.5 0.1 shard_map.77
  48.5 14.9 %all_to_all.17 = f32[64,3,4,128]{3,2,1,0:T(4,128)S(1)} all-to-all(f32[64,3,4,128]{3,2,1,0:T(4,128)S(1)} %bitcast.15), channel_id=1, replica_groups=mesh['x'=4,'y_hi'=2,'core'=2,'y_lo'=2,'z'=4] {'x','y_hi','y_lo','z'}, dimensions={0} | all-to-all | bytes 786432 | tf_op jit(solution)/shard_map/all_to_all | solution.py:245
  63.4 2.9 %collective-permute-start.1 = (f32[768,128]{1,0:T(8,128)S(1)}, f32[768,128]{1,0:T(8,128)S(1)}, u32[]{:S(2)}, u32[]{:S(2)}) collective-permute-start(f32[768,128]{1,0:T(8,128)S(1)} %bitcast.8), channel_id=1, source_target_pairs={{0,8},{8,0},{1,9},{9,1},{2,10},{10,2},{3,11},{11,3},{4,12},{12,4},... | collective-permute-start | bytes 1179656 | tf_op jit(solution)/shard_map/ppermute | solution.py:249
  66.2 0.8 %shard_map.78.placed = f32[440,440]{1,0:T(8,128)} custom-call(f32[768,128]{1,0:T(8,128)S(1)} %bitcast.9), custom_call_target="tpu_custom_call" | custom-call | flops 1000000 | bytes 4000000 | tf_op jit(solution)/shard_map/pallas_call | solution.py:323
  67.1 0.5 collective-permute-done.1.given_ref
  67.6 0.8 %shard_map.79 = f32[440,440]{1,0:T(8,128)} custom-call(f32[768,128]{1,0:T(8,128)S(1)} %bitcast.10, f32[768,128]{1,0:T(8,128)S(1)} %collective-permute-done.1.given_ref, f32[440,440]{1,0:T(8,128)} %shard_map.78.placed), custom_call_target="tpu_custom_call", output_to_operand_aliasing={{}: (2, {})} | custom-call | tf_op jit(solution)/shard_map/pallas_call | solution.py:332
Async XLA Ops:
  30.7 2.3 %collective-permute-start = (bf16[256,512]{1,0:T(8,128)(2,1)S(1)}, bf16[256,512]{1,0:T(8,128)(2,1)S(1)}, u32[]{:S(2)}, u32[]{:S(2)}) collective-permute-start(bf16[256,512]{1,0:T(8,128)(2,1)S(1)} %shard_map.74.own_ref), channel_id=1, source_target_pairs={{0,8},{8,0},{1,9},{9,1},{2,10},{10,2},{3,11},{11,3},{4,12},{12,4},... | collective-permute-start | bytes 786440 | tf_op jit(solution)/shard_map/ppermute | solution.py:249
  63.4 4.2 %collective-permute-start.1 = (f32[768,128]{1,0:T(8,128)S(1)}, f32[768,128]{1,0:T(8,128)S(1)}, u32[]{:S(2)}, u32[]{:S(2)}) collective-permute-start(f32[768,128]{1,0:T(8,128)S(1)} %bitcast.8), channel_id=1, source_target_pairs={{0,8},{8,0},{1,9},{9,1},{2,10},{10,2},{3,11},{11,3},{4,12},{12,4},... | collective-permute-start | bytes 1179656 | tf_op jit(solution)/shard_map/ppermute | solution.py:249

commit v11 on v10

--- a/solution.py
+++ b/solution.py
@@ -237,8 +237,8 @@
 def place_other_kernel(kept_ref, given_ref, placed, out_hbm, out_ref, sent):
     del placed
     core = lax.axis_index("core")
-    pl.when(core == 0)(lambda: put_rows(kept_ref, given_ref, FULL_TILES, 55, 7, out_hbm, out_ref, sent))
-    pl.when(core == 1)(lambda: put_rows(given_ref, kept_ref, 0, FULL_TILES + 1, 7, out_hbm, out_ref, sent))
+    pl.when(core == 0)(lambda: put_rows(kept_ref, given_ref, FULL_TILES, 55, 2, out_hbm, out_ref, sent))
+    pl.when(core == 1)(lambda: put_rows(given_ref, kept_ref, 0, FULL_TILES + 1, 2, out_hbm, out_ref, sent))
 
 
 def exchange(x, axes, shape):
@@ -334,7 +334,7 @@
         out_shape=density,
         in_specs=[vmem, vmem, hbm],
         out_specs=hbm,
-        scratch_shapes=[pltpu.VMEM(((FULL_TILES + 1) * 8, 440), f32), pltpu.SemaphoreType.DMA((4,))],
+        scratch_shapes=[pltpu.VMEM(((FULL_TILES + 1) * 8, 440), f32), pltpu.SemaphoreType.DMA((14,))],
         input_output_aliases={2: 0},
         compiler_params=PARAMS,
     )(slices, other_slices, placed)

time: 68.6 us -> 68.7 us (level)
  no operation moved by 1% of the time
where the time goes in v11:
time: 68.7 us; the launch traced here: 68.5 us
  blocking collectives  58 us (84%)
  Pallas kernels  5.61 us (8%)
  starting transfers between devices  3.68 us (5%)
  between operations  0.69 us (1%)
    all_to_all x3, blocking collectives, exchange(): lax.all_to_all(x.reshape(shape), axes, 0, 0, tiled=True).reshape(x.shape)  58 us
    ppermute x2, starting transfers between devices, to_other_core(): return lax.ppermute(x, 'core', [(0, 1), (1, 0)])  3.68 us
    pallas_call x1, Pallas kernels, shards(): pl.pallas_call(send_kernel, out_shape=jax.ShapeDtypeStruct((DEVICES * MES...  1.87 us
    pallas_call x1, Pallas kernels, shards(): call(times_kernel, [jax.ShapeDtypeStruct((256, 512), f32), jax.ShapeDtype...  1.46 us
  transfers between devices with their start and end apart: 2, of which 1 were waited for; matrix products, arithmetic and copies ran while one was open for 0% of the time, Pallas kernels for 3%

profile of v11, /device:TPU:1, one launch (start us, length us, event | category | flops | bytes accessed | tf_op | source)
XLA Modules:
  0.0 68.5 jit_solution(16759593083969294138)
XLA Ops:
  0.7 1.9 %shard_map.73 = bf16[3072,128]{1,0:T(8,128)(2,1)S(1)} custom-call(s32[1,1]{1,0:T(1,128)S(6)} %copy.10.counts, bf16[1,4,440,128]{3,2,1,0:T(8,128)(2,1)} %bitcast.17, bf16[1,2,440,128]{3,2,1,0:T(8,128)(2,1)} %bitcast.18, s32[1,1,128]{2,1,0:T(1,128)} %pairs_final.1, s32[1,1,128]{2,1,0:T(1,128)} %pairs_initial.1, s32[1,4,440]{2,1,0:T(4,128)} %maps_final.1, ...), custom_call_target="tpu_custom_call" | custom-call | tf_op jit(solution)/shard_map/pallas_call | solution.py:269
  2.5 28.0 %all_to_all.15 = bf16[128,24,128]{2,1,0:T(8,128)(2,1)S(1)} all-to-all(bf16[128,24,128]{2,1,0:T(8,128)(2,1)S(1)} %bitcast.13), channel_id=1, replica_groups=mesh['x'=4,'y_hi'=2,'core'=2,'y_lo'=2,'z'=4] {'x','y_hi','core','y_lo','z'}, dimensions={0} | all-to-all | bytes 1572864 | tf_op jit(solution)/shard_map/all_to_all | solution.py:245
  30.6 0.1 shard_map.74.own_ref
  30.7 0.8 %collective-permute-start = (bf16[256,512]{1,0:T(8,128)(2,1)S(1)}, bf16[256,512]{1,0:T(8,128)(2,1)S(1)}, u32[]{:S(2)}, u32[]{:S(2)}) collective-permute-start(bf16[256,512]{1,0:T(8,128)(2,1)S(1)} %shard_map.74.own_ref), channel_id=1, source_target_pairs={{0,8},{8,0},{1,9},{9,1},{2,10},{10,2},{3,11},{11,3},{4,12},{12,4},... | collective-permute-start | bytes 786440 | tf_op jit(solution)/shard_map/ppermute | solution.py:249
  31.5 1.5 %shard_map.75 = (f32[256,512]{1,0:T(8,128)S(1)}, bf16[512,256]{1,0:T(8,128)(2,1)S(1)}) custom-call(bf16[3072,128]{1,0:T(8,128)(2,1)S(1)} %bitcast.12, bf16[256,512]{1,0:T(8,128)(2,1)S(1)} %shard_map.74.own_ref), custom_call_target="tpu_custom_call" | custom-call | flops 1000000000 | bytes 8000000 | tf_op jit(solution)/shard_map/pallas_call | solution.py:304
  33.0 0.0 collective-permute-done.other_ref
  33.0 0.4 shard_map.76
  33.4 15.1 %all_to_all.16 = f32[64,3,4,128]{3,2,1,0:T(4,128)S(1)} all-to-all(f32[64,3,4,128]{3,2,1,0:T(4,128)S(1)} %bitcast.16), channel_id=1, replica_groups=mesh['x'=4,'y_hi'=2,'core'=2,'y_lo'=2,'z'=4] {'x','y_hi','y_lo','z'}, dimensions={0} | all-to-all | bytes 786432 | tf_op jit(solution)/shard_map/all_to_all | solution.py:245
  48.5 0.1 shard_map.77
  48.5 14.9 %all_to_all.17 = f32[64,3,4,128]{3,2,1,0:T(4,128)S(1)} all-to-all(f32[64,3,4,128]{3,2,1,0:T(4,128)S(1)} %bitcast.15), channel_id=1, replica_groups=mesh['x'=4,'y_hi'=2,'core'=2,'y_lo'=2,'z'=4] {'x','y_hi','y_lo','z'}, dimensions={0} | all-to-all | bytes 786432 | tf_op jit(solution)/shard_map/all_to_all | solution.py:245
  63.4 2.9 %collective-permute-start.1 = (f32[768,128]{1,0:T(8,128)S(1)}, f32[768,128]{1,0:T(8,128)S(1)}, u32[]{:S(2)}, u32[]{:S(2)}) collective-permute-start(f32[768,128]{1,0:T(8,128)S(1)} %bitcast.8), channel_id=1, source_target_pairs={{0,8},{8,0},{1,9},{9,1},{2,10},{10,2},{3,11},{11,3},{4,12},{12,4},... | collective-permute-start | bytes 1179656 | tf_op jit(solution)/shard_map/ppermute | solution.py:249
  66.2 0.8 %shard_map.78.placed = f32[440,440]{1,0:T(8,128)} custom-call(f32[768,128]{1,0:T(8,128)S(1)} %bitcast.9), custom_call_target="tpu_custom_call" | custom-call | flops 1000000 | bytes 4000000 | tf_op jit(solution)/shard_map/pallas_call | solution.py:323
  67.1 0.5 collective-permute-done.1.given_ref
  67.6 0.9 %shard_map.79 = f32[440,440]{1,0:T(8,128)} custom-call(f32[768,128]{1,0:T(8,128)S(1)} %bitcast.10, f32[768,128]{1,0:T(8,128)S(1)} %collective-permute-done.1.given_ref, f32[440,440]{1,0:T(8,128)} %shard_map.78.placed), custom_call_target="tpu_custom_call", output_to_operand_aliasing={{}: (2, {})} | custom-call | tf_op jit(solution)/shard_map/pallas_call | solution.py:332
Async XLA Ops:
  30.7 2.3 %collective-permute-start = (bf16[256,512]{1,0:T(8,128)(2,1)S(1)}, bf16[256,512]{1,0:T(8,128)(2,1)S(1)}, u32[]{:S(2)}, u32[]{:S(2)}) collective-permute-start(bf16[256,512]{1,0:T(8,128)(2,1)S(1)} %shard_map.74.own_ref), channel_id=1, source_target_pairs={{0,8},{8,0},{1,9},{9,1},{2,10},{10,2},{3,11},{11,3},{4,12},{12,4},... | collective-permute-start | bytes 786440 | tf_op jit(solution)/shard_map/ppermute | solution.py:249
  63.4 4.2 %collective-permute-start.1 = (f32[768,128]{1,0:T(8,128)S(1)}, f32[768,128]{1,0:T(8,128)S(1)}, u32[]{:S(2)}, u32[]{:S(2)}) collective-permute-start(f32[768,128]{1,0:T(8,128)S(1)} %bitcast.8), channel_id=1, source_target_pairs={{0,8},{8,0},{1,9},{9,1},{2,10},{10,2},{3,11},{11,3},{4,12},{12,4},... | collective-permute-start | bytes 1179656 | tf_op jit(solution)/shard_map/ppermute | solution.py:249
